TPU v7x, 128 devices: a whole 4x4x4 slice. The times are simulated.
128 devices in a mesh: wide: 16 (over x, z), narrow: 8 (over y, core).
Axes of the slice: x: 4, y: 4, z: 4, core: 2. Of those that a mesh axis runs over, the one named last changes fastest.
Arguments:
- grad_kv: bfloat16 [8, 576, 7168], P(None, 'wide', 'narrow'), may hold values from -60 to 60
- grad_router: bfloat16 [8, 384, 7168], P(None, 'wide', 'narrow'), may hold values from -60 to 60
- momentum: float32 [48, 576, 7168], P('wide', None, 'narrow'), may hold values from -8 to 8
- owner: int32 [16], replicated, may hold values from 0 to 15, as said below
Outputs:
- update_kv: bfloat16 [8, 576, 7168], P(None, 'wide', 'narrow')
- update_router: bfloat16 [8, 384, 7168], P(None, 'wide', 'narrow')
- new_momentum: float32 [48, 576, 7168], P('wide', None, 'narrow')
Inputs may be any that keep to these rules, and one draw needn't show every extreme that they name: Each owner index appears at most 3 times, and some index exactly 3 times.
All inputs are finite; a program needn't handle non-finite values.
Results may differ from a plain program's by a relative error of at most 0.015.
Values may be sent and summed in bfloat16 or wider, within the bound.
A program may use at most 192 MiB of HBM per device.

v0:
```python
import math

import jax
import jax.numpy as jnp
from jax import lax
from jax.sharding import PartitionSpec as P

D = 7168
NS_ITERS = 3


MOMENTUM_DECAY = 0.95
POLY_LINEAR = 3.4445
POLY_CUBIC = -4.775
POLY_QUINTIC = 2.0315
EPSILON = 1e-07
HALF_ROOT = 0.7071067811865476
FULL = lax.Precision.HIGHEST


def from_partner(value, axis, bit):
    mask = 2**bit
    pairs = [(source, source ^ mask) for source in range(lax.axis_size(axis))]
    return lax.ppermute(value, axis, pairs)


def mix_pairs(packed, narrow_count):
    position = lax.axis_index("narrow")
    current = packed
    for bit_pos in range(narrow_count.bit_length() - 1):
        partner = from_partner(current, "narrow", bit_pos)
        is_upper = position >> bit_pos & 1 == 1
        own_part = current.astype(jnp.float32)
        peer_part = partner.astype(jnp.float32)
        mixed = jnp.where(is_upper, peer_part - own_part, own_part + peer_part) * HALF_ROOT
        current = mixed.astype(jnp.bfloat16)
    return current


def local_gram(iterate):
    return jnp.einsum(
        "srd,std->srt", iterate, iterate, precision=FULL, preferred_element_type=jnp.float32
    )


def summed_gram(iterate):
    terms = local_gram(iterate)
    return jnp.stack([lax.psum(terms[slot_pos], "narrow") for slot_pos in range(terms.shape[0])])


def orthogonalize(rounded):
    start_value = rounded.astype(jnp.float32)
    first_gram = summed_gram(start_value)
    diagonal = jnp.trace(first_gram, axis1=1, axis2=2)
    inverse_norm = (1.0 / (jnp.sqrt(diagonal) + EPSILON))[:, None, None]
    iterate = inverse_norm * start_value
    current = inverse_norm * inverse_norm * first_gram
    for turn_index in range(NS_ITERS):
        if turn_index > 0:
            current = summed_gram(iterate)
        squared = jnp.einsum(
            "srt,stu->sru", current, current, precision=FULL, preferred_element_type=jnp.float32
        )
        polynomial = POLY_CUBIC * current + POLY_QUINTIC * squared
        product = jnp.einsum(
            "srt,std->srd", polynomial, iterate, precision=FULL, preferred_element_type=jnp.float32
        )
        iterate = POLY_LINEAR * iterate + product
    return iterate


def local(grad_kv, grad_router, momentum, owner):
    wide_count = lax.axis_size("wide")
    narrow_count = lax.axis_size("narrow")
    layers, kv_local, columns = grad_kv.shape
    router_local = grad_router.shape[1]
    slot_count = momentum.shape[0]
    kv_rows = momentum.shape[1]
    mat_count = owner.shape[0]
    packed = jnp.concatenate([grad_kv, grad_router], axis=1)
    rotated = mix_pairs(packed, narrow_count)
    rot_kv = rotated[:, :kv_local]
    rot_router = jnp.pad(rotated[:, kv_local:], ((0, 0), (0, kv_local - router_local), (0, 0)))
    stacked = jnp.stack([rot_kv, rot_router], axis=1).reshape(mat_count, kv_local, columns)
    matrix_ids = jnp.arange(mat_count, dtype=jnp.int32)
    same_owner = owner[None, :] == owner[:, None]
    earlier = matrix_ids[None, :] < matrix_ids[:, None]
    slot_of = jnp.sum(jnp.where(same_owner & earlier, 1, 0), axis=1).astype(jnp.int32)
    owner_range = jnp.arange(wide_count, dtype=jnp.int32)
    slot_range = jnp.arange(slot_count, dtype=jnp.int32)
    matches = (owner[None, None, :] == owner_range[:, None, None]) & (
        slot_of[None, None, :] == slot_range[None, :, None]
    )
    slot_table = jnp.sum(jnp.where(matches, matrix_ids[None, None, :], 0), axis=2)
    filled = jnp.any(matches, axis=2)
    outgoing = jnp.take(stacked, slot_table.reshape(-1), axis=0).reshape(
        wide_count, slot_count, kv_local, columns
    )
    outgoing = jnp.where(filled[:, :, None, None], outgoing, jnp.zeros((), jnp.bfloat16))
    arrived = lax.all_to_all(outgoing, "wide", split_axis=0, concat_axis=0, tiled=True)
    my_index = lax.axis_index("wide")
    my_table = lax.dynamic_index_in_dim(slot_table, my_index, 0, keepdims=False)
    my_filled = lax.dynamic_index_in_dim(filled, my_index, 0, keepdims=False)
    is_router = my_filled & (my_table % 2 == 1)
    gradients = arrived.transpose(1, 0, 2, 3).reshape(slot_count, kv_rows, columns)
    row_ids = jnp.arange(kv_rows, dtype=jnp.int32)
    router_row = row_ids < router_local * wide_count
    source_rows = jnp.where(
        router_row, row_ids // router_local * kv_local + row_ids % router_local, row_ids
    )
    reordered = jnp.where(
        router_row[None, :, None],
        jnp.take(gradients, source_rows, axis=1),
        jnp.zeros((), jnp.bfloat16),
    )
    gradients = jnp.where(is_router[:, None, None], reordered, gradients)
    valid = my_filled[:, None] & (jnp.logical_not(is_router)[:, None] | router_row[None, :])
    fresh = gradients.astype(jnp.float32)
    state = jnp.where(valid[:, :, None], MOMENTUM_DECAY * momentum + fresh, 0.0)
    push = fresh + MOMENTUM_DECAY * state
    iterate = orthogonalize(push.astype(jnp.bfloat16))
    update_gain = 0.2 * math.sqrt(D)
    update = (update_gain * iterate).astype(jnp.bfloat16)
    keep_row = row_ids % kv_local < router_local
    back_rows = jnp.where(keep_row, row_ids // kv_local * router_local + row_ids % kv_local, 0)
    router_back = jnp.where(
        keep_row[None, :, None], jnp.take(update, back_rows, axis=1), jnp.zeros((), jnp.bfloat16)
    )
    update = jnp.where(is_router[:, None, None], router_back, update)
    leaving = update.reshape(slot_count, wide_count, kv_local, columns).transpose(1, 0, 2, 3)
    returned = lax.all_to_all(leaving, "wide", split_axis=0, concat_axis=0, tiled=True)
    home = owner * slot_count + slot_of
    mine_update = jnp.take(
        returned.reshape(wide_count * slot_count, kv_local, columns), home, axis=0
    )
    mine_update = mine_update.reshape(layers, 2, kv_local, columns)
    return (mine_update[:, 0], mine_update[:, 1, :router_local], state)


def solution(mesh):
    in_specs = (
        P(None, "wide", "narrow"),
        P(None, "wide", "narrow"),
        P("wide", None, "narrow"),
        P(),
    )
    out_specs = (P(None, "wide", "narrow"), P(None, "wide", "narrow"), P("wide", None, "narrow"))
    return jax.shard_map(local, mesh=mesh, in_specs=in_specs, out_specs=out_specs, check_vma=False)
```

profile of v0, /device:TPU:93, one launch (start us, length us, event | category | flops | bytes accessed | tf_op | source)
XLA Modules:
  0.0 605.7 jit_solution(12576004576428218004)
XLA Ops:
  7.2 1.1 constant_dynamic-update-slice_fusion
  8.2 1.0 copy_dynamic-update-slice_fusion
  10.0 2.0 collective-permute-done
  13.0 0.9 select_reduce_fusion.1
  14.5 18.3 %collective-permute-done.1 = bf16[8,60,896]{2,0,1:T(8,128)(2,1)S(1)} collective-permute-done((bf16[8,60,896]{2,0,1:T(8,128)(2,1)S(1)}, bf16[8,60,896]{2,0,1:T(8,128)(2,1)S(1)}, u32[]{:S(2)}, u32[]{:S(2)}) %collective-permute-start.1) | collective-permute-done | bytes 860192 | tf_op jit(solution)/shard_map/ppermute | solution.py:24
  33.2 1.0 collective-permute-start.2
  35.0 19.2 %collective-permute-done.2 = bf16[8,60,896]{2,0,1:T(8,128)(2,1)S(1)} collective-permute-done((bf16[8,60,896]{2,0,1:T(8,128)(2,1)S(1)}, bf16[8,60,896]{2,0,1:T(8,128)(2,1)S(1)}, u32[]{:S(2)}, u32[]{:S(2)}) %collective-permute-start.2) | collective-permute-done | bytes 860192 | tf_op jit(solution)/shard_map/ppermute | solution.py:24
  55.0 3.0 gather_fusion
  58.0 4.4 select_select_fusion
  62.3 6.8 %all-to-all-start = ((bf16[16,3,36,896]{3,2,1,0:T(8,128)(2,1)}), bf16[16,3,36,896]{3,2,1,0:T(8,128)(2,1)S(1)}, u32[]{:S(2)}, u32[]{:S(2)}) async-start(bf16[16,3,36,896]{3,2,1,0:T(8,128)(2,1)} %select_select_fusion), calls=%async_computation | async-start | bytes 6881280 | tf_op jit(solution)/shard_map/all_to_all | solution.py:100
  70.3 38.2 %all-to-all-done = bf16[16,3,36,896]{3,2,1,0:T(8,128)(2,1)S(1)} async-done(((bf16[16,3,36,896]{3,2,1,0:T(8,128)(2,1)}), bf16[16,3,36,896]{3,2,1,0:T(8,128)(2,1)S(1)}, u32[]{:S(2)}, u32[]{:S(2)}) %all-to-all-start) | async-done | bytes 3096608 | tf_op jit(solution)/shard_map/all_to_all | solution.py:100
  108.5 2.0 copy.64
  110.5 3.7 reshape.252
  114.3 4.6 copy.65
  118.9 10.7 %gather_fusion.2 = bf16[576,3,896]{2,1,0:T(4,128)(2,1)} fusion(bf16[3,576,896]{2,0,1:T(4,128)(2,1)} %copy.65, s32[1024]{0:T(1024)S(1)} %pad_clamp_fusion.2), kind=kCustom, calls=%fused_computation.clone | custom fusion | bytes 6195456 | tf_op jit(solution)/shard_map/jit(_take)/gather | solution.py:113
  129.6 5.5 fusion
  135.1 2.9 fusion.71
  138.7 2.1 fusion.78
  141.2 78.3 %all-reduce.12.cloned.1.call-done = (f32[1,576,576]{2,1,0:T(8,128)}, f32[1,576,576]{2,1,0:T(8,128)}, f32[1,576,576]{2,1,0:T(8,128)}) async-done(((f32[1,576,576]{2,1,0:T(8,128)}, f32[1,576,576]{2,1,0:T(8,128)}, f32[1,576,576]{2,1,0:T(8,128)}), (f32[1,576,576]{2,1,0:T(8,128)}, f32[1,576,576]{2,1,0:T(8,128)}, f32[1,576,576]{2,1,0:T(8,128)})) %all-reduce.12.cloned.1.call-update) | async-done | bytes 3981328 | tf_op jit(solution)/shard_map/psum | solution.py:48
  219.5 1.6 constant_dynamic-update-slice_fusion.3
  221.1 1.5 constant_dynamic-update-slice_fusion.2
  222.7 0.9 select_reduce_fusion
  223.6 13.2 %fusion.14 = f32[3,576,576]{2,1,0:T(8,128)S(1)} fusion(f32[3,576,576]{2,1,0:T(8,128)S(1)} %constant_dynamic-update-slice_fusion.1, f32[3]{0:T(128)S(1)} %get-tuple-element.16), kind=kOutput, calls=%fused_computation.25 | convolution fusion | flops 6880702464 | bytes 7962636 | tf_op jit(solution)/shard_map/srt,stu->sru/dot_general | solution.py:61
  236.8 18.8 %multiply_add_fusion.1 = f32[3,576,896]{2,1,0:T(8,128)S(1)} fusion(f32[3,576,576]{2,1,0:T(8,128)S(1)} %fusion.14, f32[3,576,576]{2,1,0:T(8,128)S(1)} %constant_dynamic-update-slice_fusion.1, f32[3]{0:T(128)S(1)} %get-tuple-element.17, f32[3]{0:T(128)S(1)} %get-tuple-element.16, f32[3,576,896]{2,1,0:T(8,128)S(1)} %bitcast.43, ...), kind=kOutput, calls=%fused_computation.10 | convolution fusion | flops 10727424000 | bytes 23445528 | tf_op jit(solution)/shard_map/srt,std->srd/dot_general | solution.py:65
  255.6 16.8 %fusion.79 = f32[3,576,576]{2,1,0:T(8,128)S(1)} fusion(f32[3,576,896]{2,1,0:T(8,128)S(1)} %multiply_add_fusion.1), kind=kOutput, calls=%fused_computation.146 | convolution fusion | flops 10701766656 | bytes 10174464 | tf_op jit(solution)/shard_map/srd,std->srt/dot_general | solution.py:41
  272.4 2.2 fusion.77
  274.8 73.6 %all-reduce.10.cloned.1.call-done = (f32[1,576,576]{2,1,0:T(8,128)}, f32[1,576,576]{2,1,0:T(8,128)}, f32[1,576,576]{2,1,0:T(8,128)}) async-done(((f32[1,576,576]{2,1,0:T(8,128)}, f32[1,576,576]{2,1,0:T(8,128)}, f32[1,576,576]{2,1,0:T(8,128)}), (f32[1,576,576]{2,1,0:T(8,128)}, f32[1,576,576]{2,1,0:T(8,128)}, f32[1,576,576]{2,1,0:T(8,128)})) %all-reduce.10.cloned.1.call-update) | async-done | bytes 3981328 | tf_op jit(solution)/shard_map/psum | solution.py:48
  348.4 1.6 constant_dynamic-update-slice_fusion.6
  350.0 1.5 constant_dynamic-update-slice_fusion.5
  351.6 12.7 %fusion.80 = f32[3,576,576]{2,1,0:T(8,128)S(1)} fusion(f32[3,576,576]{2,1,0:T(8,128)S(1)} %constant_dynamic-update-slice_fusion.4), kind=kOutput, calls=%fused_computation.147 | convolution fusion | flops 6879707136 | bytes 7962624 | tf_op jit(solution)/shard_map/srt,stu->sru/dot_general | solution.py:61
  364.3 18.0 %multiply_add_fusion = f32[3,576,896]{2,1,0:T(8,128)S(1)} fusion(f32[3,576,896]{2,1,0:T(8,128)S(1)} %bitcast.41, f32[3,576,576]{2,1,0:T(8,128)S(1)} %fusion.80, f32[3,576,576]{2,1,0:T(8,128)S(1)} %constant_dynamic-update-slice_fusion.4), kind=kOutput, calls=%fused_computation.9 | convolution fusion | flops 10707849216 | bytes 20348928 | tf_op jit(solution)/shard_map/srt,std->srd/dot_general | solution.py:65
  382.4 17.0 %fusion.81 = f32[3,576,576]{2,1,0:T(8,128)S(1)} fusion(f32[3,576,896]{2,1,0:T(8,128)S(1)} %multiply_add_fusion), kind=kOutput, calls=%fused_computation.148 | convolution fusion | flops 10701766656 | bytes 10174464 | tf_op jit(solution)/shard_map/srd,std->srt/dot_general | solution.py:41
  399.3 2.2 fusion.76
  401.6 73.8 %all-reduce.8.cloned.1.call-done = (f32[1,576,576]{2,1,0:T(8,128)}, f32[1,576,576]{2,1,0:T(8,128)}, f32[1,576,576]{2,1,0:T(8,128)}) async-done(((f32[1,576,576]{2,1,0:T(8,128)}, f32[1,576,576]{2,1,0:T(8,128)}, f32[1,576,576]{2,1,0:T(8,128)}), (f32[1,576,576]{2,1,0:T(8,128)}, f32[1,576,576]{2,1,0:T(8,128)}, f32[1,576,576]{2,1,0:T(8,128)})) %all-reduce.8.cloned.1.call-update) | async-done | bytes 3981328 | tf_op jit(solution)/shard_map/psum | solution.py:48
  475.4 1.6 constant_dynamic-update-slice_fusion.9
  477.0 1.5 constant_dynamic-update-slice_fusion.8
  478.6 13.0 %fusion.82 = f32[3,576,576]{2,1,0:T(8,128)S(1)} fusion(f32[3,576,576]{2,1,0:T(8,128)S(1)} %constant_dynamic-update-slice_fusion.7), kind=kOutput, calls=%fused_computation.149 | convolution fusion | flops 6879707136 | bytes 7962624 | tf_op jit(solution)/shard_map/srt,stu->sru/dot_general | solution.py:61
  491.6 17.5 %multiply_convert_fusion = bf16[3,576,896]{2,1,0:T(8,128)(2,1)S(1)} fusion(f32[3,576,896]{2,1,0:T(8,128)S(1)} %bitcast.39, f32[3,576,576]{2,1,0:T(8,128)S(1)} %fusion.82, f32[3,576,576]{2,1,0:T(8,128)S(1)} %constant_dynamic-update-slice_fusion.7), kind=kOutput, calls=%fused_computation.8 | convolution fusion | flops 10710945792 | bytes 17252352 | tf_op jit(solution)/shard_map/srt,std->srd/dot_general | solution.py:65
  509.0 4.6 copy.67
  513.7 10.9 %gather_fusion.3 = bf16[576,3,896]{2,1,0:T(4,128)(2,1)} fusion(bf16[3,576,896]{2,0,1:T(4,128)(2,1)} %copy.67, s32[1024]{0:T(1024)S(1)} %pad_clamp_fusion.1), kind=kCustom, calls=%fused_computation.1.clone | custom fusion | bytes 6195456 | tf_op jit(solution)/shard_map/jit(_take)/gather | solution.py:127
  524.6 4.8 fusion.21
  529.3 3.7 reshape.253
  533.0 2.0 copy.69
  535.0 6.8 %all-to-all-start.1 = ((bf16[16,3,36,896]{3,2,1,0:T(8,128)(2,1)}), bf16[16,3,36,896]{3,2,1,0:T(8,128)(2,1)S(1)}, u32[]{:S(2)}, u32[]{:S(2)}) async-start(bf16[16,3,36,896]{3,2,1,0:T(8,128)(2,1)} %copy.69), calls=%async_computation.1 | async-start | bytes 6881280 | tf_op jit(solution)/shard_map/all_to_all | solution.py:131
  541.9 50.3 %all-to-all-done.1 = bf16[16,3,36,896]{3,2,1,0:T(8,128)(2,1)S(1)} async-done(((bf16[16,3,36,896]{3,2,1,0:T(8,128)(2,1)}), bf16[16,3,36,896]{3,2,1,0:T(8,128)(2,1)S(1)}, u32[]{:S(2)}, u32[]{:S(2)}) %all-to-all-start.1) | async-done | bytes 3096608 | tf_op jit(solution)/shard_map/all_to_all | solution.py:131
  592.2 1.7 gather_fusion.1
  593.9 2.4 broadcast_select_fusion
  597.9 0.8 copy.87
  (79 shorter events, 8.6 us)
Async XLA Ops:
  9.3 2.8 collective-permute-start
  12.4 20.4 %collective-permute-start.1 = (bf16[8,60,896]{2,0,1:T(8,128)(2,1)S(1)}, bf16[8,60,896]{2,0,1:T(8,128)(2,1)S(1)}, u32[]{:S(2)}, u32[]{:S(2)}) collective-permute-start(bf16[8,60,896]{2,0,1:T(8,128)(2,1)S(1)} %fusion.36), channel_id=1, source_target_pairs={{0,2},{1,3},{2,0},{3,1},{4,6},{5,7},{6,4},{7,5},{8,10},{9,11},{10,... | collective-permute-start | bytes 2580488 | tf_op jit(solution)/shard_map/ppermute | solution.py:24
  33.2 21.0 %collective-permute-start.2 = (bf16[8,60,896]{2,0,1:T(8,128)(2,1)S(1)}, bf16[8,60,896]{2,0,1:T(8,128)(2,1)S(1)}, u32[]{:S(2)}, u32[]{:S(2)}) collective-permute-start(bf16[8,60,896]{2,0,1:T(8,128)(2,1)S(1)} %fusion.39), channel_id=1, source_target_pairs={{0,4},{1,5},{2,6},{3,7},{4,0},{5,1},{6,2},{7,3},{8,12},{9,13},{10,... | collective-permute-start | bytes 2580488 | tf_op jit(solution)/shard_map/ppermute | solution.py:24
  62.3 46.1 %all-to-all-start = ((bf16[16,3,36,896]{3,2,1,0:T(8,128)(2,1)}), bf16[16,3,36,896]{3,2,1,0:T(8,128)(2,1)S(1)}, u32[]{:S(2)}, u32[]{:S(2)}) async-start(bf16[16,3,36,896]{3,2,1,0:T(8,128)(2,1)} %select_select_fusion), calls=%async_computation | async-start | bytes 6881280 | tf_op jit(solution)/shard_map/all_to_all | solution.py:100
  69.2 150.3 %all-reduce.12.cloned.1.call-start = ((), (), s32[]{:S(2)}) async-start(), calls=%async_computation.4 | async-start | bytes 8847360 | tf_op jit(solution)/shard_map/psum | solution.py:48
  135.1 2.9 copy-start.2
  135.1 3.7 copy-start.3
  140.9 207.5 %all-reduce.10.cloned.1.call-start = ((), (), s32[]{:S(2)}) async-start(), calls=%async_computation.3 | async-start | bytes 8847360 | tf_op jit(solution)/shard_map/psum | solution.py:48
  219.5 3.1 copy-start.6
  222.7 14.1 %slice-start.4 = ((s8[6193152]{0:T(1024)(128)(4,1)}), s8[4194304]{0:T(1024)(128)(4,1)S(1)}, s32[]{:S(2)}) async-start(s8[6193152]{0:T(1024)(128)(4,1)} %bitcast.42), calls=%async_computation.9 | async-start | bytes 8388608
  223.5 13.2 %slice-start.5 = ((s8[6193152]{0:T(1024)(128)(4,1)}), s8[1998848]{0:T(1024)(128)(4,1)S(1)}, s32[]{:S(2)}) async-start(s8[6193152]{0:T(1024)(128)(4,1)} %bitcast.42), calls=%async_computation.10 | async-start | bytes 3997696
  223.5 13.2 %copy-start.4 = (bf16[3,576,896]{2,1,0:T(8,128)(2,1)S(1)}, bf16[3,576,896]{2,1,0:T(8,128)(2,1)}, u32[]{:S(2)}) copy-start(bf16[3,576,896]{2,1,0:T(8,128)(2,1)} %copy-done.3) | copy-start | bytes 9289732
  255.6 16.8 %copy-start.1 = (f32[3,576,896]{2,1,0:T(8,128)}, f32[3,576,896]{2,1,0:T(8,128)S(1)}, u32[]{:S(2)}) copy-start(f32[3,576,896]{2,1,0:T(8,128)S(1)} %multiply_add_fusion.1) | copy-start | bytes 18579460
  274.6 200.8 %all-reduce.8.cloned.1.call-start = ((), (), s32[]{:S(2)}) async-start(), calls=%async_computation.2 | async-start | bytes 8847360 | tf_op jit(solution)/shard_map/psum | solution.py:48
  348.4 3.1 copy-start.7
  351.4 12.9 %slice-start.2 = ((s8[6193152]{0:T(1024)(128)(4,1)}), s8[4194304]{0:T(1024)(128)(4,1)S(1)}, s32[]{:S(2)}) async-start(s8[6193152]{0:T(1024)(128)(4,1)} %bitcast.40), calls=%async_computation.7 | async-start | bytes 8388608
  351.6 12.8 %slice-start.3 = ((s8[6193152]{0:T(1024)(128)(4,1)}), s8[1998848]{0:T(1024)(128)(4,1)S(1)}, s32[]{:S(2)}) async-start(s8[6193152]{0:T(1024)(128)(4,1)} %bitcast.40), calls=%async_computation.8 | async-start | bytes 3997696
  382.3 17.0 %copy-start = (f32[3,576,896]{2,1,0:T(8,128)}, f32[3,576,896]{2,1,0:T(8,128)S(1)}, u32[]{:S(2)}) copy-start(f32[3,576,896]{2,1,0:T(8,128)S(1)} %multiply_add_fusion) | copy-start | bytes 18579460
  475.4 3.1 copy-start.5
  478.4 13.1 %slice-start = ((s8[6193152]{0:T(1024)(128)(4,1)}), s8[4194304]{0:T(1024)(128)(4,1)S(1)}, s32[]{:S(2)}) async-start(s8[6193152]{0:T(1024)(128)(4,1)} %bitcast.38), calls=%async_computation.5 | async-start | bytes 8388608
  478.6 13.0 %slice-start.1 = ((s8[6193152]{0:T(1024)(128)(4,1)}), s8[1998848]{0:T(1024)(128)(4,1)S(1)}, s32[]{:S(2)}) async-start(s8[6193152]{0:T(1024)(128)(4,1)} %bitcast.38), calls=%async_computation.6 | async-start | bytes 3997696
  535.0 6.8 %copy-start.8 = (s32[16]{0:T(128)S(1)}, s32[16]{0:T(128)}, u32[]{:S(2)}) copy-start(s32[16]{0:T(128)} %param.9) | copy-start | bytes 196
  535.0 57.3 %all-to-all-start.1 = ((bf16[16,3,36,896]{3,2,1,0:T(8,128)(2,1)}), bf16[16,3,36,896]{3,2,1,0:T(8,128)(2,1)S(1)}, u32[]{:S(2)}, u32[]{:S(2)}) async-start(bf16[16,3,36,896]{3,2,1,0:T(8,128)(2,1)} %copy.69), calls=%async_computation.1 | async-start | bytes 6881280 | tf_op jit(solution)/shard_map/all_to_all | solution.py:131
Sparse Core Ops, SparseCore 0:
  141.0 78.4 all-reduce.11
  274.7 73.6 all-reduce.9
  401.7 73.6 all-reduce.7
where the time goes:
time: 610 us; the launch traced here: 606 us
  waiting for transfers between devices  354 us (58%)
  matrix products  130 us (21%)
  local copies, waits for them, and re-layouts  69.3 us (11%)
  other arithmetic  21.2 us (3%)
  starting transfers between devices  16.9 us (3%)
  between operations  14.7 us (2%)
    psum x3, waiting for transfers between devices, summed_gram(): lax.psum(terms[slot_pos], 'narrow')  226 us
    dot_general x3, matrix products, orthogonalize(): jnp.einsum('srt,std->srd', polynomial, iterate, precision=FULL, preferred...  54.2 us
    all_to_all x1, waiting for transfers between devices, local(): lax.all_to_all(leaving, 'wide', split_axis=0, concat_axis=0, tiled=True)  50.3 us
    ppermute x3, waiting for transfers between devices, from_partner(): return lax.ppermute(value, axis, pairs)  39.6 us
    dot_general x3, matrix products, orthogonalize(): jnp.einsum('srt,stu->sru', current, current, precision=FULL, preferred_el...  38.9 us
    all_to_all x1, waiting for transfers between devices, local(): lax.all_to_all(outgoing, 'wide', split_axis=0, concat_axis=0, tiled=True)  38.2 us
    dot_general x3, matrix products, local_gram(): jnp.einsum('srd,std->srt', iterate, iterate, precision=FULL, preferred_el...  36.6 us
  transfers between devices with their start and end apart: 8, of which 8 were waited for; matrix products, arithmetic and copies ran while one was open for 1% of the time, Pallas kernels for 0%

commit v1 on v0

v1 whole, which is shorter than its diff:
```python
import math

import jax
import jax.numpy as jnp
from jax import lax
from jax.experimental import pallas as pl
from jax.experimental.pallas import tpu as pltpu
from jax.sharding import PartitionSpec as P

D = 7168
KV = 576
EX = 384
LAYERS = 8
MATS = 16
MOST = 3
WIDE = 16
NARROW = 8
COLS = D // NARROW
KVL = KV // WIDE
EXL = EX // WIDE
BLK = 128
PADDED = 640

MOMENTUM_DECAY = 0.95
POLY_LINEAR = 3.4445
POLY_CUBIC = -4.775
POLY_QUINTIC = 2.0315
EPSILON = 1e-07
HALF_ROOT = 0.7071067811865476
GAIN = 0.2 * math.sqrt(D)

MESH = pl.DeviceIdType.MESH
F32 = jnp.float32
BF16 = jnp.bfloat16


def hops(offset):
    return sum(min(step, 4 - step) for step in offset)


WIDE_OFFSETS = sorted(
    [(i, j) for i in range(4) for j in range(4) if i or j], key=lambda o: -hops(o)
)
NARROW_OFFSETS = [(2, 0), (2, 1), (1, 0), (3, 0), (1, 1), (3, 1), (0, 1)]
UPPER = [(i, j) for i in range(5) for j in range(i, 5)]


def split(value):
    high = value.astype(BF16)
    low = (value - high.astype(F32)).astype(BF16)
    return high, low


def product(left, right):
    left_high, left_low = left
    right_high, right_low = right
    return jnp.dot(
        jnp.concatenate([left_high, left_high, left_low], axis=1),
        jnp.concatenate([right_high, right_low, right_high], axis=0),
        preferred_element_type=F32,
    )


def step_kernel(
    gkv,
    gr,
    mom_hbm,
    owner,
    out_kv,
    out_r,
    ma,
    momv,
    msend,
    marr,
    rk,
    rr,
    tk,
    tr,
    mk,
    mr,
    m36,
    ms,
    xk,
    xr,
    xak,
    xar,
    xmat,
    gb,
    ga,
    gh,
    gn,
    full,
    umat,
    uk,
    ur,
    slot_ref,
    load_sem,
    rot_send,
    rot_recv,
    back_send,
    back_recv,
    mom_send,
    mom_recv,
    x_send,
    x_recv,
    own_send,
    own_recv,
    own_local,
    red_send,
    red_recv,
    out_send,
    out_recv,
):
    w = lax.axis_index("wide")
    n = lax.axis_index("narrow")
    x, z = w // 4, w % 4
    y, c = n // 2, n % 2

    def wide_peer(offset, sign=1):
        return ((x + 4 + sign * offset[0]) % 4) * 4 + (z + 4 + sign * offset[1]) % 4

    def narrow_peer(offset, sign=1):
        return ((y + 4 + sign * offset[0]) % 4) * 2 + (c + offset[1]) % 2

    def remote(src, dst, send, recv, where):
        return pltpu.make_async_remote_copy(
            src_ref=src,
            dst_ref=dst,
            send_sem=send,
            recv_sem=recv,
            device_id=where,
            device_id_type=MESH,
        )

    loads = [
        pltpu.make_async_copy(mom_hbm.at[s], momv.at[s], load_sem.at[s]) for s in range(MOST)
    ]
    for load in loads:
        load.start()

    barrier = pltpu.get_barrier_semaphore()
    for offset in WIDE_OFFSETS:
        pl.semaphore_signal(
            barrier, inc=1, device_id={"wide": wide_peer(offset)}, device_id_type=MESH
        )
    for offset in NARROW_OFFSETS:
        pl.semaphore_signal(
            barrier, inc=1, device_id={"narrow": narrow_peer(offset)}, device_id_type=MESH
        )
    pl.semaphore_wait(barrier, len(WIDE_OFFSETS) + len(NARROW_OFFSETS))

    rot = []
    for i, offset in enumerate(NARROW_OFFSETS):
        to = narrow_peer(offset)
        for part, (src, dst) in enumerate(((gkv, rk), (gr, rr))):
            copy = remote(
                src.at[to],
                dst.at[n],
                rot_send.at[part, i],
                rot_recv.at[part, i],
                {"narrow": to},
            )
            copy.start()
            rot.append(copy)
    rk[n] = gkv[n]
    rr[n] = gr[n]

    owners = [owner[k] for k in range(MATS)]
    slots = []
    for k in range(MATS):
        taken = jnp.int32(0)
        for before in range(k):
            taken = taken + jnp.where(owners[before] == owners[k], 1, 0)
        slots.append(taken)
        slot_ref[k] = taken

    mom = []
    for s in range(MOST):
        odd = jnp.int32(0)
        for k in range(1, MATS, 2):
            odd = odd + jnp.where((owners[k] == w) & (slots[k] == s), 1, 0)
        loads[s].wait()
        is_router = jnp.full((KVL, COLS), odd, jnp.int32) == 1
        for j in range(WIDE):
            as_kv = momv[s, j * KVL : (j + 1) * KVL, :]
            as_router = momv[s, j * EXL : j * EXL + KVL, :]
            msend[s, j] = jnp.where(is_router, as_router, as_kv).astype(BF16)
        for i, offset in enumerate(WIDE_OFFSETS):
            to = wide_peer(offset)
            copy = remote(
                msend.at[s, to],
                marr.at[w, s],
                mom_send.at[s, i],
                mom_recv.at[s, i],
                {"wide": to},
            )
            copy.start()
            mom.append(copy)
        marr[w, s] = msend[s, w]

    def rotate(source, target):
        def column(t, carry):
            cols = pl.ds(pl.multiple_of(t * BLK, BLK), BLK)
            blocks = [source[b, :, cols].astype(F32) for b in range(NARROW)]
            for bit in range(3):
                stride = 1 << bit
                mixed = list(blocks)
                for b in range(NARROW):
                    if not b & stride:
                        low, high = blocks[b], blocks[b + stride]
                        mixed[b] = ((low + high) * HALF_ROOT).astype(BF16)
                        mixed[b + stride] = ((low - high) * HALF_ROOT).astype(BF16)
                        if bit < 2:
                            mixed[b] = mixed[b].astype(F32)
                            mixed[b + stride] = mixed[b + stride].astype(F32)
                blocks = mixed
            for b in range(NARROW):
                target[b, :, cols] = blocks[b]
            return carry

        lax.fori_loop(0, COLS // BLK, column, 0)

    back = []
    for part, (arrived, turned, final) in enumerate(((rk, tk, mk), (rr, tr, mr))):
        for i, offset in enumerate(NARROW_OFFSETS):
            rot[2 * i + part].wait_recv()
        rotate(arrived, turned)
        for i, offset in enumerate(NARROW_OFFSETS):
            to = narrow_peer(offset)
            copy = remote(
                turned.at[to],
                final.at[n],
                back_send.at[part, i],
                back_recv.at[part, i],
                {"narrow": to},
            )
            copy.start()
            back.append(copy)
        final[n] = turned[n]
    for copy in back:
        copy.wait_recv()
    for copy in mom:
        copy.wait_recv()

    def push(layer, carry):
        for part, (source, target, rows) in enumerate(((mk, xk, KVL), (mr, xr, EXL))):
            k = 2 * layer + part
            held = marr[owner[k], jnp.minimum(slot_ref[k], MOST - 1)][:rows].astype(F32)
            rounded = source[layer]
            fresh = rounded.astype(F32)
            state = MOMENTUM_DECAY * held + fresh
            target[layer] = (fresh + MOMENTUM_DECAY * state).astype(BF16)
            m36[k, 0:rows, :] = rounded
        return carry

    lax.fori_loop(0, LAYERS, push, 0)

    def x_copies(i, offset):
        to = wide_peer(offset)
        even = remote(
            xk.at[to // 2], xak.at[w], x_send.at[i], x_recv.at[i], {"wide": to}
        )
        odd = remote(xr.at[to // 2], xar.at[w], x_send.at[i], x_recv.at[i], {"wide": to})
        return to, even, odd

    is_even = w % 2 == 0
    for i, offset in enumerate(WIDE_OFFSETS):
        to, even, odd = x_copies(i, offset)

        @pl.when(to % 2 == 0)
        def _():
            even.start()

        @pl.when(to % 2 == 1)
        def _():
            odd.start()

    def stage(o, carry):
        for s in range(MOST):
            held = jnp.int32(0)
            for k in range(MATS):
                held = held + jnp.where((owner[k] == o) & (slot_ref[k] == s), k, 0)
            ms[s, o] = m36[held]
        return carry

    lax.fori_loop(0, WIDE, stage, 0)
    own = []
    for s in range(MOST):
        for i, offset in enumerate(WIDE_OFFSETS):
            to = wide_peer(offset)
            copy = remote(
                ms.at[s, to], ma.at[s, w], own_send.at[s, i], own_recv.at[s, i], {"wide": to}
            )
            copy.start()
            own.append(copy)
    stays = [pltpu.make_async_copy(ms.at[s, w], ma.at[s, w], own_local.at[s]) for s in range(MOST)]
    for copy in stays:
        copy.start()

    @pl.when(is_even)
    def _():
        xak[w] = xk[w // 2]
        for i, offset in enumerate(WIDE_OFFSETS):
            x_copies(i, offset)[1].wait_recv()
        for j in range(WIDE):
            xmat[j * KVL : (j + 1) * KVL, :] = xak[j].astype(F32)
        xmat[KV:, :] = jnp.zeros((PADDED - KV, COLS), F32)

    @pl.when(jnp.logical_not(is_even))
    def _():
        xar[w] = xr[w // 2]
        for i, offset in enumerate(WIDE_OFFSETS):
            x_copies(i, offset)[2].wait_recv()
        for j in range(WIDE):
            xmat[j * EXL : (j + 1) * EXL, :] = xar[j].astype(F32)
        xmat[EX:, :] = jnp.zeros((PADDED - EX, COLS), F32)

    values = xmat[...].astype(BF16)
    gram = lax.dot_general(
        values, values, (((1,), (1,)), ((), ())), preferred_element_type=F32
    )
    for b, (i, j) in enumerate(UPPER):
        gb[b] = gram[i * BLK : (i + 1) * BLK, j * BLK : (j + 1) * BLK]
    gb[15] = jnp.zeros((BLK, BLK), F32)

    partner = {"narrow": y * 2 + 1 - c}
    pair = remote(
        gb.at[pl.ds((1 - c) * 8, 8)], ga, red_send.at[0], red_recv.at[0], partner
    )
    pair.start()
    pair.wait_recv()
    gh[...] = gb[pl.ds(c * 8, 8)] + ga[...]
    scatter = []
    for i, step in enumerate((2, 1, 3)):
        to = (y + step) % 4
        copy = remote(
            gh.at[pl.ds(to * 2, 2)],
            gn.at[i],
            red_send.at[1 + i],
            red_recv.at[1 + i],
            {"narrow": to * 2 + c},
        )
        copy.start()
        scatter.append(copy)
    for copy in scatter:
        copy.wait_recv()
    mine = pl.ds(c * 8 + y * 2, 2)
    full[mine] = gh[pl.ds(y * 2, 2)] + gn[0] + gn[1] + gn[2]
    gather = []
    for i, step in enumerate((2, 1, 3)):
        to = (y + step) % 4
        copy = remote(
            full.at[mine],
            full.at[mine],
            red_send.at[4 + i],
            red_recv.at[4 + i],
            {"narrow": to * 2 + c},
        )
        copy.start()
        gather.append(copy)
    for copy in gather:
        copy.wait_recv()
    half = pl.ds(c * 8, 8)
    final_pair = remote(full.at[half], full.at[half], red_send.at[7], red_recv.at[7], partner)
    final_pair.start()
    final_pair.wait_recv()

    blocks = {}
    trace = jnp.zeros((1, 1), F32)
    eye = (
        lax.broadcasted_iota(jnp.int32, (BLK, BLK), 0)
        == lax.broadcasted_iota(jnp.int32, (BLK, BLK), 1)
    )
    for b, (i, j) in enumerate(UPPER):
        block = full[b]
        blocks[i, j] = block
        if i == j:
            trace = trace + jnp.sum(jnp.where(eye, block, 0.0), keepdims=True)
        else:
            blocks[j, i] = block.T
    first = jnp.concatenate(
        [jnp.concatenate([blocks[i, j] for j in range(5)], axis=1) for i in range(5)], axis=0
    )[:KV, :KV]
    inverse_norm = 1.0 / (jnp.sqrt(trace) + EPSILON)
    current = inverse_norm * inverse_norm * first

    diagonal = (
        lax.broadcasted_iota(jnp.int32, (KV, KV), 0)
        == lax.broadcasted_iota(jnp.int32, (KV, KV), 1)
    )

    def polynomial(gram_value, parts):
        return POLY_CUBIC * gram_value + POLY_QUINTIC * product(parts, parts)

    weight = None
    for turn in range(3):
        parts = split(current)
        cubic = split(polynomial(current, parts))
        if turn == 0:
            weight = jnp.where(diagonal, POLY_LINEAR, 0.0) + (
                cubic[0].astype(F32) + cubic[1].astype(F32)
            )
        else:
            weight = POLY_LINEAR * weight + product(cubic, split(weight))
        if turn < 2:
            half_way = POLY_LINEAR * current + product(cubic, parts)
            current = POLY_LINEAR * half_way + product(cubic, split(half_way))
    weight = split(weight * (inverse_norm * GAIN))
    weights = jnp.concatenate(weight, axis=1)
    values = values[:KV]
    umat[...] = jnp.dot(
        weights, jnp.concatenate([values, values], axis=0), preferred_element_type=F32
    )

    layer = w // 2

    def out_copies(i, offset):
        to = wide_peer(offset)
        where = {"wide": to}
        even = remote(uk.at[to], out_kv.at[layer], out_send.at[i], out_recv.at[i], where)
        odd = remote(ur.at[to], out_r.at[layer], out_send.at[i], out_recv.at[i], where)
        return even, odd

    @pl.when(is_even)
    def _():
        for j in range(WIDE):
            uk[j] = umat[j * KVL : (j + 1) * KVL, :].astype(BF16)
        for i, offset in enumerate(WIDE_OFFSETS):
            out_copies(i, offset)[0].start()
        out_kv[layer] = uk[w]

    @pl.when(jnp.logical_not(is_even))
    def _():
        for j in range(WIDE):
            ur[j] = umat[j * EXL : (j + 1) * EXL, :].astype(BF16)
        for i, offset in enumerate(WIDE_OFFSETS):
            out_copies(i, offset)[1].start()
        out_r[layer] = ur[w]

    for i, offset in enumerate(WIDE_OFFSETS):
        source = wide_peer(offset, -1)
        where = {"wide": wide_peer(offset)}
        even = remote(
            uk.at[0], out_kv.at[source // 2], out_send.at[i], out_recv.at[i], where
        )
        odd = remote(ur.at[0], out_r.at[source // 2], out_send.at[i], out_recv.at[i], where)

        @pl.when(source % 2 == 0)
        def _():
            even.wait_recv()

        @pl.when(source % 2 == 1)
        def _():
            odd.wait_recv()

    for copy in own:
        copy.wait_recv()
    for copy in stays:
        copy.wait()
    for copy in rot + back + mom + own + scatter + gather + [pair, final_pair]:
        copy.wait_send()
    for i, offset in enumerate(WIDE_OFFSETS):
        to, even, odd = x_copies(i, offset)

        @pl.when(to % 2 == 0)
        def _():
            even.wait_send()

        @pl.when(to % 2 == 1)
        def _():
            odd.wait_send()

    @pl.when(is_even)
    def _():
        for i, offset in enumerate(WIDE_OFFSETS):
            out_copies(i, offset)[0].wait_send()

    @pl.when(jnp.logical_not(is_even))
    def _():
        for i, offset in enumerate(WIDE_OFFSETS):
            out_copies(i, offset)[1].wait_send()


def state_kernel(owner, mom, ma, out):
    w = lax.axis_index("wide")
    s = pl.program_id(0)
    kind = jnp.int32(0)
    for k in range(MATS):
        slot = jnp.int32(0)
        for before in range(k):
            slot = slot + jnp.where(owner[before] == owner[k], 1, 0)
        kind = kind + jnp.where((owner[k] == w) & (slot == s), 1 + k % 2, 0)

    @pl.when(kind == 1)
    def _():
        for j in range(WIDE):
            rows = slice(j * KVL, (j + 1) * KVL)
            out[0, rows, :] = MOMENTUM_DECAY * mom[0, rows, :] + ma[0, j].astype(F32)

    @pl.when(kind == 2)
    def _():
        for j in range(WIDE):
            rows = slice(j * EXL, (j + 1) * EXL)
            out[0, rows, :] = MOMENTUM_DECAY * mom[0, rows, :] + ma[0, j, :EXL].astype(F32)
        out[0, EX:, :] = jnp.zeros((KV - EX, COLS), F32)

    @pl.when(kind == 0)
    def _():
        out[...] = jnp.zeros((1, KV, COLS), F32)


def local(grad_kv, grad_router, momentum, owner):
    vmem = pl.BlockSpec(memory_space=pltpu.VMEM)
    hbm = pl.BlockSpec(memory_space=pl.ANY)
    smem = pl.BlockSpec(memory_space=pltpu.SMEM)
    dma = pltpu.SemaphoreType.DMA
    kv_blocks = lambda count: pltpu.VMEM((count, KVL, COLS), BF16)
    r_blocks = lambda count: pltpu.VMEM((count, EXL, COLS), BF16)
    square = lambda count: pltpu.VMEM((count, BLK, BLK), F32)
    update_kv, update_router, arrived = pl.pallas_call(
        step_kernel,
        out_shape=(
            jax.ShapeDtypeStruct((LAYERS, KVL, COLS), BF16),
            jax.ShapeDtypeStruct((LAYERS, EXL, COLS), BF16),
            jax.ShapeDtypeStruct((MOST, WIDE, KVL, COLS), BF16),
        ),
        in_specs=[vmem, vmem, hbm, smem],
        out_specs=(vmem, vmem, hbm),
        scratch_shapes=[
            pltpu.VMEM((MOST, KV, COLS), F32),
            pltpu.VMEM((MOST, WIDE, KVL, COLS), BF16),
            pltpu.VMEM((WIDE, MOST, KVL, COLS), BF16),
            kv_blocks(NARROW),
            r_blocks(NARROW),
            kv_blocks(NARROW),
            r_blocks(NARROW),
            kv_blocks(LAYERS),
            r_blocks(LAYERS),
            kv_blocks(MATS),
            pltpu.VMEM((MOST, WIDE, KVL, COLS), BF16),
            kv_blocks(LAYERS),
            r_blocks(LAYERS),
            kv_blocks(WIDE),
            r_blocks(WIDE),
            pltpu.VMEM((PADDED, COLS), F32),
            square(16),
            square(8),
            square(8),
            pltpu.VMEM((3, 2, BLK, BLK), F32),
            square(16),
            pltpu.VMEM((KV, COLS), F32),
            kv_blocks(WIDE),
            r_blocks(WIDE),
            pltpu.SMEM((MATS,), jnp.int32),
            dma((MOST,)),
            dma((2, 7)),
            dma((2, 7)),
            dma((2, 7)),
            dma((2, 7)),
            dma((MOST, 15)),
            dma((MOST, 15)),
            dma((15,)),
            dma((15,)),
            dma((MOST, 15)),
            dma((MOST, 15)),
            dma((MOST,)),
            dma((8,)),
            dma((8,)),
            dma((15,)),
            dma((15,)),
        ],
        compiler_params=pltpu.CompilerParams(
            collective_id=0, has_side_effects=True, vmem_limit_bytes=60 * 2**20
        ),
        name="step",
    )(grad_kv, grad_router, momentum, owner)
    new_momentum = pl.pallas_call(
        state_kernel,
        grid=(MOST,),
        out_shape=jax.ShapeDtypeStruct((MOST, KV, COLS), F32),
        in_specs=[
            smem,
            pl.BlockSpec((1, KV, COLS), lambda s: (s, 0, 0)),
            pl.BlockSpec((1, WIDE, KVL, COLS), lambda s: (s, 0, 0, 0)),
        ],
        out_specs=pl.BlockSpec((1, KV, COLS), lambda s: (s, 0, 0)),
        compiler_params=pltpu.CompilerParams(vmem_limit_bytes=32 * 2**20),
        name="state",
    )(owner, momentum, arrived)
    return update_kv, update_router, new_momentum


def solution(mesh):
    in_specs = (
        P(None, "wide", "narrow"),
        P(None, "wide", "narrow"),
        P("wide", None, "narrow"),
        P(),
    )
    out_specs = (P(None, "wide", "narrow"), P(None, "wide", "narrow"), P("wide", None, "narrow"))
    return jax.shard_map(local, mesh=mesh, in_specs=in_specs, out_specs=out_specs, check_vma=False)
```

time: 610 us -> 154 us (0.25)
  the two profiles are of different devices: /device:TPU:93 before, /device:TPU:1 now
where the time goes in v1:
time: 154 us; the launch traced here: 151 us
  Pallas kernels  142 us (92%)
  local copies, waits for them, and re-layouts  9.28 us (6%)
    pallas_call x1, Pallas kernels, local(): pl.pallas_call(step_kernel, out_shape=(jax.ShapeDtypeStruct((LAYERS, KVL,...  138 us
    unnamed x11, local copies, waits for them, and re-layouts  9.28 us
    pallas_call x1, Pallas kernels, local(): pl.pallas_call(state_kernel, grid=(MOST,), out_shape=jax.ShapeDtypeStruct...  3.83 us

profile of v1, /device:TPU:1, one launch (start us, length us, event | category | flops | bytes accessed | tf_op | source)
XLA Modules:
  0.0 151.4 jit_solution(15995989484363416329)
XLA Ops:
  0.6 0.0 copy-start.2
  0.6 1.9 %copy.7.gkv = bf16[8,36,896]{2,1,0:T(8,128)(2,1)} copy(bf16[8,36,896]{2,0,1:T(8,128)(2,1)} %param.4) | data formatting | bytes 1032192 | tf_op args[0]
  2.6 137.7 %step.1 = (bf16[8,36,896]{2,1,0:T(8,128)(2,1)}, bf16[8,24,896]{2,1,0:T(8,128)(2,1)}, bf16[3,16,36,896]{3,2,1,0:T(8,128)(2,1)}) custom-call(bf16[8,36,896]{2,1,0:T(8,128)(2,1)} %copy.7.gkv, bf16[8,24,896]{2,1,0:T(8,128)(2,1)} %gr.1, f32[3,576,896]{2,1,0:T(8,128)} %mom.1, s32[16]{0:T(128)} %owner.3), custom_call_target="tpu_custom_call" | custom-call | tf_op jit(solution)/shard_map/step/pallas_call | solution.py:520
  140.2 1.9 %copy.8 = bf16[8,36,896]{2,0,1:T(8,128)(2,1)} copy(bf16[8,36,896]{2,1,0:T(8,128)(2,1)} %get-tuple-element.9) | data formatting | bytes 1032192
  142.1 0.0 copy-done.2
  142.1 0.0 copy-start
  142.1 2.8 %copy-done = f32[3,576,896]{2,1,0:T(8,128)S(1)} copy-done((f32[3,576,896]{2,1,0:T(8,128)S(1)}, f32[3,576,896]{2,1,0:T(8,128)}, u32[]{:S(2)}) %copy-start) | copy-done | bytes 6193176
  144.9 0.0 copy-start.1
  144.9 2.0 %copy-done.1 = bf16[3,16,36,896]{3,2,1,0:T(8,128)(2,1)S(1)} copy-done((bf16[3,16,36,896]{3,2,1,0:T(8,128)(2,1)S(1)}, bf16[3,16,36,896]{3,2,1,0:T(8,128)(2,1)}, u32[]{:S(2)}) %copy-start.1) | copy-done | bytes 3096600
  146.9 0.0 copy-start.3
  146.9 3.8 %state.1 = f32[3,576,896]{2,1,0:T(8,128)} custom-call(s32[16]{0:T(128)S(1)} %copy-done.2, f32[3,576,896]{2,1,0:T(8,128)S(1)} %copy-done, bf16[3,16,36,896]{3,2,1,0:T(8,128)(2,1)S(1)} %copy-done.1), custom_call_target="tpu_custom_call" | custom-call | tf_op jit(solution)/shard_map/state/pallas_call | solution.py:577
  150.7 0.0 copy-done.3
  150.7 0.7 copy.10
Async XLA Ops:
  0.6 141.5 %copy-start.2 = (s32[16]{0:T(128)S(1)}, s32[16]{0:T(128)}, u32[]{:S(2)}) copy-start(s32[16]{0:T(128)} %owner.3) | copy-start | bytes 196
  142.1 2.8 %copy-start = (f32[3,576,896]{2,1,0:T(8,128)S(1)}, f32[3,576,896]{2,1,0:T(8,128)}, u32[]{:S(2)}) copy-start(f32[3,576,896]{2,1,0:T(8,128)} %mom.1) | copy-start | bytes 18579460
  144.9 2.0 %copy-start.1 = (bf16[3,16,36,896]{3,2,1,0:T(8,128)(2,1)S(1)}, bf16[3,16,36,896]{3,2,1,0:T(8,128)(2,1)}, u32[]{:S(2)}) copy-start(bf16[3,16,36,896]{3,2,1,0:T(8,128)(2,1)} %get-tuple-element.8.ma) | copy-start | bytes 9289732
  146.9 3.8 %copy-start.3 = (bf16[8,24,896]{2,1,0:T(8,128)(2,1)S(1)}, bf16[8,24,896]{2,1,0:T(8,128)(2,1)}, u32[]{:S(2)}) copy-start(bf16[8,24,896]{2,1,0:T(8,128)(2,1)} %get-tuple-element.16) | copy-start | bytes 1032196

commit v2 on v1

v2 whole, which is shorter than its diff:
```python
import math

import jax
import jax.numpy as jnp
from jax import lax
from jax.experimental import pallas as pl
from jax.experimental.pallas import tpu as pltpu
from jax.sharding import PartitionSpec as P

D = 7168
KV = 576
EX = 384
LAYERS = 8
MATS = 16
MOST = 3
WIDE = 16
NARROW = 8
COLS = D // NARROW
KVL = KV // WIDE
EXL = EX // WIDE
BLK = 128
PADDED = 640
ROWS = 32
LANES = COLS + BLK
TILES = COLS // BLK
TAIL = KVL - ROWS

MOMENTUM_DECAY = 0.95
POLY_LINEAR = 3.4445
POLY_CUBIC = -4.775
POLY_QUINTIC = 2.0315
EPSILON = 1e-07
HALF_ROOT = 0.7071067811865476
GAIN = 0.2 * math.sqrt(D)

MESH = pl.DeviceIdType.MESH
F32 = jnp.float32
BF16 = jnp.bfloat16


def hops(offset):
    return sum(min(step, 4 - step) for step in offset)


WIDE_OFFSETS = sorted(
    [(i, j) for i in range(4) for j in range(4) if i or j], key=lambda o: -hops(o)
)
NARROW_OFFSETS = [(2, 0), (2, 1), (1, 0), (3, 0), (1, 1), (3, 1), (0, 1)]
UPPER = [(i, j) for i in range(5) for j in range(i, 5)]


def split(value):
    high = value.astype(BF16)
    low = (value - high.astype(F32)).astype(BF16)
    return high, low


def product(left, right):
    left_high, left_low = left
    right_high, right_low = right
    return jnp.dot(
        jnp.concatenate([left_high, left_high, left_low], axis=1),
        jnp.concatenate([right_high, right_low, right_high], axis=0),
        preferred_element_type=F32,
    )


def step_kernel(
    gkv,
    gr,
    mom_hbm,
    owner,
    out_kv,
    out_r,
    ma,
    momv,
    msend,
    marr,
    gp,
    rk,
    rr,
    tk,
    tr,
    mk,
    mr,
    mats,
    ms,
    xk,
    xr,
    xak,
    xar,
    xmat,
    xtail,
    tails,
    gb,
    ga,
    gh,
    gn,
    full,
    wmat,
    uk,
    ur,
    slot_ref,
    load_sem,
    rot_send,
    rot_recv,
    back_send,
    back_recv,
    mom_send,
    mom_recv,
    x_send,
    x_recv,
    own_send,
    own_recv,
    own_local,
    red_send,
    red_recv,
    out_send,
    out_recv,
):
    w = lax.axis_index("wide")
    n = lax.axis_index("narrow")
    x, z = w // 4, w % 4
    y, c = n // 2, n % 2
    is_even = w % 2 == 0
    is_odd = w % 2 == 1

    def wide_peer(offset):
        return ((x + offset[0]) % 4) * 4 + (z + offset[1]) % 4

    def narrow_peer(offset):
        return ((y + offset[0]) % 4) * 2 + (c + offset[1]) % 2

    def remote(src, dst, send, recv, where):
        return pltpu.make_async_remote_copy(
            src_ref=src,
            dst_ref=dst,
            send_sem=send,
            recv_sem=recv,
            device_id=where,
            device_id_type=MESH,
        )

    next_wide = {"wide": wide_peer((0, 1))}
    next_narrow = {"narrow": narrow_peer((0, 1))}

    def arrived(ref, sem, where):
        remote(ref, ref, sem, sem, where).wait_recv()

    def sent(ref, sem, where):
        remote(ref, ref, sem, sem, where).wait_send()

    loads = [
        pltpu.make_async_copy(mom_hbm.at[s], momv.at[s], load_sem.at[s]) for s in range(MOST)
    ]
    for load in loads:
        load.start()

    barrier = pltpu.get_barrier_semaphore()
    for offset in WIDE_OFFSETS:
        pl.semaphore_signal(
            barrier, inc=1, device_id={"wide": wide_peer(offset)}, device_id_type=MESH
        )
    for offset in NARROW_OFFSETS:
        pl.semaphore_signal(
            barrier, inc=1, device_id={"narrow": narrow_peer(offset)}, device_id_type=MESH
        )

    owners = [owner[k] for k in range(MATS)]
    slots = []
    for k in range(MATS):
        taken = jnp.int32(0)
        for before in range(k):
            taken = taken + jnp.where(owners[before] == owners[k], 1, 0)
        slots.append(taken)
        slot_ref[k] = taken

    tails[...] = jnp.zeros(tails.shape, F32)

    def pack_momentum(s):
        odd = jnp.int32(0)
        for k in range(1, MATS, 2):
            odd = odd + jnp.where((owners[k] == w) & (slots[k] == s), 1, 0)
        loads[s].wait()
        is_router = jnp.full((ROWS, COLS), odd, jnp.int32) == 1
        for j in range(WIDE):
            as_kv = momv[s, j * KVL : j * KVL + ROWS, :]
            as_router = momv[s, j * EXL : j * EXL + ROWS, :]
            msend[s, j, :, :COLS] = jnp.where(is_router, as_router, as_kv).astype(BF16)
            rest = momv[s, j * KVL + ROWS : (j + 1) * KVL, :]
            for t in range(TILES):
                tails[j, t * TAIL : (t + 1) * TAIL, :] = rest[:, t * BLK : (t + 1) * BLK]
        msend[s, :, :, COLS:] = tails[...].astype(BF16)

    def send_momentum(s):
        for offset in WIDE_OFFSETS:
            to = wide_peer(offset)
            remote(
                msend.at[s, to], marr.at[w, s], mom_send.at[0], mom_recv.at[0], {"wide": to}
            ).start()
        marr[w, s] = msend[s, w]

    pack_momentum(0)
    pl.semaphore_wait(barrier, len(WIDE_OFFSETS) + len(NARROW_OFFSETS))
    send_momentum(0)

    def gather_columns(part, source, target):
        for offset in NARROW_OFFSETS:
            to = narrow_peer(offset)
            remote(
                source.at[to], target.at[n], rot_send.at[part], rot_recv.at[part], {"narrow": to}
            ).start()
        target[n] = source[n]

    gather_columns(1, gr, rr)
    for t in range(TILES):
        cols = slice(t * BLK, (t + 1) * BLK)
        by_layer = jnp.swapaxes(gkv[:, :, cols].astype(F32), 0, 1)
        gp[:, :, cols] = by_layer[:, :ROWS].astype(BF16)
        tails[:LAYERS, t * TAIL : (t + 1) * TAIL, :] = by_layer[:, ROWS:]
    gp[:, :, COLS:] = tails[:LAYERS].astype(BF16)
    gather_columns(0, gp, rk)

    for s in range(1, MOST):
        pack_momentum(s)
        send_momentum(s)

    def rotate(source, target, count):
        def column(t, carry):
            cols = pl.ds(pl.multiple_of(t * BLK, BLK), BLK)
            blocks = [source[b, :, cols].astype(F32) for b in range(NARROW)]
            for bit in range(3):
                stride = 1 << bit
                mixed = list(blocks)
                for b in range(NARROW):
                    if not b & stride:
                        low, high = blocks[b], blocks[b + stride]
                        mixed[b] = ((low + high) * HALF_ROOT).astype(BF16)
                        mixed[b + stride] = ((low - high) * HALF_ROOT).astype(BF16)
                        if bit < 2:
                            mixed[b] = mixed[b].astype(F32)
                            mixed[b + stride] = mixed[b + stride].astype(F32)
                blocks = mixed
            for b in range(NARROW):
                target[b, :, cols] = blocks[b]
            return carry

        lax.fori_loop(0, count, column, 0)

    for part, source, turned, final in ((1, rr, tr, mr), (0, rk, tk, mk)):
        arrived(source.at[pl.ds(0, NARROW - 1)], rot_recv.at[part], next_narrow)
        rotate(source, turned, source.shape[2] // BLK)
        for offset in NARROW_OFFSETS:
            to = narrow_peer(offset)
            remote(
                turned.at[to], final.at[n], back_send.at[part], back_recv.at[part], {"narrow": to}
            ).start()
        final[n] = turned[n]
    for part, final in ((1, mr), (0, mk)):
        arrived(final.at[pl.ds(0, NARROW - 1)], back_recv.at[part], next_narrow)

    mats[...] = jnp.zeros(mats.shape, BF16)

    def by_matrix(layer, carry):
        mats[2 * layer] = mk[layer]
        mats[2 * layer + 1, :EXL, :COLS] = mr[layer]
        return carry

    lax.fori_loop(0, LAYERS, by_matrix, 0)

    def stage(o, carry):
        for s in range(MOST):
            held = jnp.int32(0)
            for k in range(MATS):
                held = held + jnp.where((owner[k] == o) & (slot_ref[k] == s), k, 0)
            ms[s, o] = mats[held]
        return carry

    lax.fori_loop(0, WIDE, stage, 0)
    arrived(marr.at[pl.ds(0, WIDE - 1)], mom_recv.at[0], next_wide)

    def push(layer, carry):
        for part, (source, target) in enumerate(((mk, xk), (mr, xr))):
            k = 2 * layer + part
            held = marr[owner[k], jnp.minimum(slot_ref[k], MOST - 1)]
            if part:
                held = held[:EXL, :COLS]
            fresh = source[layer].astype(F32)
            state = MOMENTUM_DECAY * held.astype(F32) + fresh
            target[layer] = (fresh + MOMENTUM_DECAY * state).astype(BF16)
        return carry

    lax.fori_loop(0, LAYERS, push, 0)

    for offset in WIDE_OFFSETS:
        to = wide_peer(offset)

        @pl.when(to % 2 == 0)
        def _():
            remote(
                xk.at[to // 2], xak.at[w], x_send.at[0], x_recv.at[0], {"wide": to}
            ).start()

        @pl.when(to % 2 == 1)
        def _():
            remote(
                xr.at[to // 2], xar.at[w], x_send.at[1], x_recv.at[0], {"wide": to}
            ).start()

    xmat[...] = jnp.zeros(xmat.shape, BF16)
    xtail[...] = jnp.zeros(xtail.shape, F32)

    @pl.when(is_even)
    def _():
        xak[w] = xk[w // 2]
        arrived(xak.at[pl.ds(0, WIDE - 1)], x_recv.at[0], next_wide)
        for j in range(WIDE):
            xmat[j * ROWS : (j + 1) * ROWS, :] = xak[j, :, :COLS]
            rest = xak[j, :, COLS:].astype(F32)
            for t in range(TILES):
                xtail[j * TAIL : (j + 1) * TAIL, t * BLK : (t + 1) * BLK] = rest[
                    t * TAIL : (t + 1) * TAIL
                ]
        xmat[WIDE * ROWS :, :] = xtail[...].astype(BF16)

    @pl.when(is_odd)
    def _():
        xar[w] = xr[w // 2]
        arrived(xar.at[pl.ds(0, WIDE - 1)], x_recv.at[0], next_wide)
        for j in range(WIDE):
            xmat[j * ROWS : j * ROWS + EXL, :] = xar[j]

    for s in range(MOST):
        for offset in WIDE_OFFSETS:
            to = wide_peer(offset)
            remote(
                ms.at[s, to], ma.at[s, w], own_send.at[0], own_recv.at[0], {"wide": to}
            ).start()
    stays = pltpu.make_async_copy(ms.at[:, w], ma.at[:, w], own_local.at[0])
    stays.start()

    gram = lax.dot_general(
        xmat[...], xmat[...], (((1,), (1,)), ((), ())), preferred_element_type=F32
    )
    for b, (i, j) in enumerate(UPPER):
        gb[b] = gram[i * BLK : (i + 1) * BLK, j * BLK : (j + 1) * BLK]
    gb[15] = jnp.zeros((BLK, BLK), F32)

    partner = {"narrow": y * 2 + 1 - c}
    pair = remote(
        gb.at[pl.ds((1 - c) * 8, 8)], ga, red_send.at[0], red_recv.at[0], partner
    )
    pair.start()
    pair.wait_recv()
    gh[...] = gb[pl.ds(c * 8, 8)] + ga[...]
    scatter = []
    for i, step in enumerate((2, 1, 3)):
        to = (y + step) % 4
        copy = remote(
            gh.at[pl.ds(to * 2, 2)],
            gn.at[i],
            red_send.at[1 + i],
            red_recv.at[1 + i],
            {"narrow": to * 2 + c},
        )
        copy.start()
        scatter.append(copy)
    for copy in scatter:
        copy.wait_recv()
    mine = pl.ds(c * 8 + y * 2, 2)
    full[mine] = gh[pl.ds(y * 2, 2)] + gn[0] + gn[1] + gn[2]
    gather = []
    for i, step in enumerate((2, 1, 3)):
        to = (y + step) % 4
        copy = remote(
            full.at[mine],
            full.at[mine],
            red_send.at[4 + i],
            red_recv.at[4 + i],
            {"narrow": to * 2 + c},
        )
        copy.start()
        gather.append(copy)
    for copy in gather:
        copy.wait_recv()
    half = pl.ds(c * 8, 8)
    final_pair = remote(full.at[half], full.at[half], red_send.at[7], red_recv.at[7], partner)
    final_pair.start()
    final_pair.wait_recv()

    blocks = {}
    trace = jnp.zeros((1, 1), F32)
    eye = (
        lax.broadcasted_iota(jnp.int32, (BLK, BLK), 0)
        == lax.broadcasted_iota(jnp.int32, (BLK, BLK), 1)
    )
    for b, (i, j) in enumerate(UPPER):
        block = full[b]
        blocks[i, j] = block
        if i == j:
            trace = trace + jnp.sum(jnp.where(eye, block, 0.0), keepdims=True)
        else:
            blocks[j, i] = block.T
    first = jnp.concatenate(
        [jnp.concatenate([blocks[i, j] for j in range(5)], axis=1) for i in range(5)], axis=0
    )[:KV, :KV]
    inverse_norm = 1.0 / (jnp.sqrt(trace) + EPSILON)
    current = inverse_norm * inverse_norm * first

    diagonal = (
        lax.broadcasted_iota(jnp.int32, (KV, KV), 0)
        == lax.broadcasted_iota(jnp.int32, (KV, KV), 1)
    )
    weight = None
    for turn in range(3):
        parts = split(current)
        cubic = split(POLY_CUBIC * current + POLY_QUINTIC * product(parts, parts))
        if turn == 0:
            weight = jnp.where(diagonal, POLY_LINEAR, 0.0) + (
                cubic[0].astype(F32) + cubic[1].astype(F32)
            )
        else:
            weight = POLY_LINEAR * weight + product(cubic, split(weight))
        if turn < 2:
            half_way = POLY_LINEAR * current + product(cubic, parts)
            current = POLY_LINEAR * half_way + product(cubic, split(half_way))
    wmat[...] = jnp.concatenate(split(weight * (inverse_norm * GAIN)), axis=1)

    layer = w // 2

    def apply(rows):
        values = xmat[:KV]
        return jnp.dot(
            wmat[rows, :], jnp.concatenate([values, values], axis=0), preferred_element_type=F32
        )

    @pl.when(is_even)
    def _():
        last = apply(pl.ds(WIDE * ROWS, WIDE * TAIL))
        for j in range(WIDE):
            for t in range(TILES):
                tails[j, t * TAIL : (t + 1) * TAIL, :] = last[
                    j * TAIL : (j + 1) * TAIL, t * BLK : (t + 1) * BLK
                ]
        uk[:, :, COLS:] = tails[...].astype(BF16)

    def outgoing(step, carry):
        group = (x + 2 + step) % 4
        chunk = apply(pl.ds(pl.multiple_of(group * BLK, BLK), BLK)).astype(BF16)
        for i in range(4):
            to = group * 4 + i
            rows = chunk[i * ROWS : (i + 1) * ROWS]

            @pl.when(is_even)
            def _():
                uk[to, :, :COLS] = rows

            @pl.when(is_odd)
            def _():
                ur[to] = rows[:EXL]

            @pl.when(jnp.logical_and(is_even, to != w))
            def _():
                remote(
                    uk.at[to], out_kv.at[layer], out_send.at[0], out_recv.at[0], {"wide": to}
                ).start()

            @pl.when(jnp.logical_and(is_odd, to != w))
            def _():
                remote(
                    ur.at[to], out_r.at[layer], out_send.at[0], out_recv.at[1], {"wide": to}
                ).start()

        return carry

    lax.fori_loop(0, 4, outgoing, 0)

    @pl.when(is_even)
    def _():
        out_kv[layer] = uk[w]
        arrived(out_kv.at[pl.ds(0, 7)], out_recv.at[0], next_wide)
        arrived(out_r.at[pl.ds(0, 8)], out_recv.at[1], next_wide)
        sent(uk.at[pl.ds(0, 15)], out_send.at[0], next_wide)
        sent(xk.at[pl.ds(0, 7)], x_send.at[0], next_wide)
        sent(xr.at[pl.ds(0, 8)], x_send.at[1], next_wide)

    @pl.when(is_odd)
    def _():
        out_r[layer] = ur[w]
        arrived(out_kv.at[pl.ds(0, 8)], out_recv.at[0], next_wide)
        arrived(out_r.at[pl.ds(0, 7)], out_recv.at[1], next_wide)
        sent(ur.at[pl.ds(0, 15)], out_send.at[0], next_wide)
        sent(xk.at[pl.ds(0, 8)], x_send.at[0], next_wide)
        sent(xr.at[pl.ds(0, 7)], x_send.at[1], next_wide)

    arrived(ma.at[:, pl.ds(0, WIDE - 1)], own_recv.at[0], next_wide)
    stays.wait()
    sent(ms.at[:, pl.ds(0, WIDE - 1)], own_send.at[0], next_wide)
    sent(msend.at[:, pl.ds(0, WIDE - 1)], mom_send.at[0], next_wide)
    for part, source, turned in ((0, gp, tk), (1, gr, tr)):
        sent(source.at[pl.ds(0, NARROW - 1)], rot_send.at[part], next_narrow)
        sent(turned.at[pl.ds(0, NARROW - 1)], back_send.at[part], next_narrow)
    for copy in scatter + gather + [pair, final_pair]:
        copy.wait_send()


def state_kernel(owner, mom, ma, out_kv, out_r, new, kv, router):
    w = lax.axis_index("wide")
    s = pl.program_id(0)
    kind = jnp.int32(0)
    for k in range(MATS):
        slot = jnp.int32(0)
        for before in range(k):
            slot = slot + jnp.where(owner[before] == owner[k], 1, 0)
        kind = kind + jnp.where((owner[k] == w) & (slot == s), 1 + k % 2, 0)

    @pl.when(kind == 1)
    def _():
        for j in range(WIDE):
            rows = slice(j * KVL, j * KVL + ROWS)
            new[0, rows, :] = MOMENTUM_DECAY * mom[0, rows, :] + ma[0, j, :, :COLS].astype(F32)
            rest = ma[0, j, :, COLS:].astype(F32)
            rows = slice(j * KVL + ROWS, (j + 1) * KVL)
            for t in range(TILES):
                cols = slice(t * BLK, (t + 1) * BLK)
                new[0, rows, cols] = (
                    MOMENTUM_DECAY * mom[0, rows, cols] + rest[t * TAIL : (t + 1) * TAIL]
                )

    @pl.when(kind == 2)
    def _():
        for j in range(WIDE):
            rows = slice(j * EXL, (j + 1) * EXL)
            new[0, rows, :] = MOMENTUM_DECAY * mom[0, rows, :] + ma[0, j, :EXL, :COLS].astype(F32)
        new[0, EX:, :] = jnp.zeros((KV - EX, COLS), F32)

    @pl.when(kind == 0)
    def _():
        new[...] = jnp.zeros((1, KV, COLS), F32)

    @pl.when(s == 0)
    def _():
        router[...] = out_r[...]
        for t in range(TILES):
            cols = slice(t * BLK, (t + 1) * BLK)
            kv[:ROWS, :, cols] = jnp.swapaxes(out_kv[:, :, cols].astype(F32), 0, 1).astype(BF16)
            rest = out_kv[:, :, COLS:].astype(F32)[:, t * TAIL : (t + 1) * TAIL]
            kv[ROWS:, :, cols] = jnp.swapaxes(rest, 0, 1).astype(BF16)


def local(grad_kv, grad_router, momentum, owner):
    vmem = pl.BlockSpec(memory_space=pltpu.VMEM)
    hbm = pl.BlockSpec(memory_space=pl.ANY)
    smem = pl.BlockSpec(memory_space=pltpu.SMEM)
    dma = pltpu.SemaphoreType.DMA
    kv_blocks = lambda *count: pltpu.VMEM(count + (ROWS, LANES), BF16)
    r_blocks = lambda count: pltpu.VMEM((count, EXL, COLS), BF16)
    square = lambda *count: pltpu.VMEM(count + (BLK, BLK), F32)
    update_kv, update_router, arrived = pl.pallas_call(
        step_kernel,
        out_shape=(
            jax.ShapeDtypeStruct((LAYERS, ROWS, LANES), BF16),
            jax.ShapeDtypeStruct((LAYERS, EXL, COLS), BF16),
            jax.ShapeDtypeStruct((MOST, WIDE, ROWS, LANES), BF16),
        ),
        in_specs=[vmem, vmem, hbm, smem],
        out_specs=(vmem, vmem, hbm),
        scratch_shapes=[
            pltpu.VMEM((MOST, KV, COLS), F32),
            kv_blocks(MOST, WIDE),
            kv_blocks(WIDE, MOST),
            kv_blocks(LAYERS),
            kv_blocks(NARROW),
            r_blocks(NARROW),
            kv_blocks(NARROW),
            r_blocks(NARROW),
            kv_blocks(LAYERS),
            r_blocks(LAYERS),
            kv_blocks(MATS),
            kv_blocks(MOST, WIDE),
            kv_blocks(LAYERS),
            r_blocks(LAYERS),
            kv_blocks(WIDE),
            r_blocks(WIDE),
            pltpu.VMEM((PADDED, COLS), BF16),
            pltpu.VMEM((PADDED - WIDE * ROWS, COLS), F32),
            pltpu.VMEM((WIDE, ROWS, BLK), F32),
            square(16),
            square(8),
            square(8),
            square(3, 2),
            square(16),
            pltpu.VMEM((KV, 2 * KV), BF16),
            kv_blocks(WIDE),
            r_blocks(WIDE),
            pltpu.SMEM((MATS,), jnp.int32),
            dma((MOST,)),
            dma((2,)),
            dma((2,)),
            dma((2,)),
            dma((2,)),
            dma((1,)),
            dma((1,)),
            dma((2,)),
            dma((1,)),
            dma((1,)),
            dma((1,)),
            dma((1,)),
            dma((8,)),
            dma((8,)),
            dma((1,)),
            dma((2,)),
        ],
        compiler_params=pltpu.CompilerParams(
            collective_id=0, has_side_effects=True, vmem_limit_bytes=60 * 2**20
        ),
        name="step",
    )(jnp.swapaxes(grad_kv, 0, 1), grad_router, momentum, owner)
    whole = lambda shape: pl.BlockSpec(shape, lambda s: (0,) * len(shape))
    new_momentum, kv, router = pl.pallas_call(
        state_kernel,
        grid=(MOST,),
        out_shape=(
            jax.ShapeDtypeStruct((MOST, KV, COLS), F32),
            jax.ShapeDtypeStruct((KVL, LAYERS, COLS), BF16),
            jax.ShapeDtypeStruct((LAYERS, EXL, COLS), BF16),
        ),
        in_specs=[
            smem,
            pl.BlockSpec((1, KV, COLS), lambda s: (s, 0, 0)),
            pl.BlockSpec((1, WIDE, ROWS, LANES), lambda s: (s, 0, 0, 0)),
            whole((LAYERS, ROWS, LANES)),
            whole((LAYERS, EXL, COLS)),
        ],
        out_specs=(
            pl.BlockSpec((1, KV, COLS), lambda s: (s, 0, 0)),
            whole((KVL, LAYERS, COLS)),
            whole((LAYERS, EXL, COLS)),
        ),
        compiler_params=pltpu.CompilerParams(vmem_limit_bytes=60 * 2**20),
        name="state",
    )(owner, momentum, arrived, update_kv, update_router)
    return jnp.swapaxes(kv, 0, 1), router, new_momentum


def solution(mesh):
    in_specs = (
        P(None, "wide", "narrow"),
        P(None, "wide", "narrow"),
        P("wide", None, "narrow"),
        P(),
    )
    out_specs = (P(None, "wide", "narrow"), P(None, "wide", "narrow"), P("wide", None, "narrow"))
    return jax.shard_map(local, mesh=mesh, in_specs=in_specs, out_specs=out_specs, check_vma=False)
```

time: 154 us -> 122 us (0.79); the launches traced: 151 us -> 122 us
  Pallas kernels: 142 us -> 121 us
  local copies, waits for them, and re-layouts: 9.28 us -> 0 us
    pallas_call x2, Pallas kernels: 142 us -> 121 us  [the longest x1 113 us: local(): pl.pallas_call(step_kernel, out_shape=(jax.ShapeDtypeStruct((LAYERS, ROWS...]
    unnamed x11 -> x0, local copies, waits for them, and re-layouts: 9.28 us -> none
where the time goes in v2:
time: 122 us
  Pallas kernels  121 us (99%)
    pallas_call x1, Pallas kernels, local(): pl.pallas_call(step_kernel, out_shape=(jax.ShapeDtypeStruct((LAYERS, ROWS...  113 us
    pallas_call x1, Pallas kernels, local(): pl.pallas_call(state_kernel, grid=(MOST,), out_shape=(jax.ShapeDtypeStruc...  8.17 us

profile of v2, /device:TPU:1, one launch (start us, length us, event | category | flops | bytes accessed | tf_op | source)
XLA Modules:
  0.0 121.7 jit_solution(13453754753050599515)
XLA Ops:
  0.6 112.8 %step.1 = (bf16[8,32,1024]{2,1,0:T(8,128)(2,1)}, bf16[8,24,896]{2,1,0:T(8,128)(2,1)}, bf16[3,16,32,1024]{3,2,1,0:T(8,128)(2,1)}) custom-call(bf16[36,8,896]{2,1,0:T(8,128)(2,1)} %bitcast.2, bf16[8,24,896]{2,1,0:T(8,128)(2,1)} %gr.1, f32[3,576,896]{2,1,0:T(8,128)} %mom.1, s32[16]{0:T(128)} %owner.3), custom_call_target="tpu_custom_call" | custom-call | tf_op jit(solution)/shard_map/step/pallas_call | solution.py:559
  113.4 8.2 %state.1 = (f32[3,576,896]{2,1,0:T(8,128)}, bf16[36,8,896]{2,1,0:T(8,128)(2,1)}, bf16[8,24,896]{2,1,0:T(8,128)(2,1)}) custom-call(s32[16]{0:T(128)} %owner.3, f32[3,576,896]{2,1,0:T(8,128)} %mom.1, bf16[3,16,32,1024]{3,2,1,0:T(8,128)(2,1)} %get-tuple-element.9.ma, bf16[8,32,1024]{2,1,0:T(8,128)(2,1)} %get-tuple-element.10.out_kv, ...), custom_call_target="tpu_custom_call" | custom-call | tf_op jit(solution)/shard_map/state/pallas_call | solution.py:620

commit v3 on v2

--- a/solution.py
+++ b/solution.py
@@ -55,12 +55,12 @@
     return high, low
 
 
-def product(left, right):
-    left_high, left_low = left
-    right_high, right_low = right
+def product(left, right, terms=3):
+    lefts = [left[0], left[0], left[1]][:terms]
+    rights = [right[0], right[1], right[0]][:terms]
     return jnp.dot(
-        jnp.concatenate([left_high, left_high, left_low], axis=1),
-        jnp.concatenate([right_high, right_low, right_high], axis=0),
+        jnp.concatenate(lefts, axis=1),
+        jnp.concatenate(rights, axis=0),
         preferred_element_type=F32,
     )
 
@@ -314,6 +314,23 @@
     def _():
         xak[w] = xk[w // 2]
         arrived(xak.at[pl.ds(0, WIDE - 1)], x_recv.at[0], next_wide)
+
+    @pl.when(is_odd)
+    def _():
+        xar[w] = xr[w // 2]
+        arrived(xar.at[pl.ds(0, WIDE - 1)], x_recv.at[0], next_wide)
+
+    for s in range(MOST):
+        for offset in WIDE_OFFSETS:
+            to = wide_peer(offset)
+            remote(
+                ms.at[s, to], ma.at[s, w], own_send.at[0], own_recv.at[0], {"wide": to}
+            ).start()
+    stays = pltpu.make_async_copy(ms.at[:, w], ma.at[:, w], own_local.at[0])
+    stays.start()
+
+    @pl.when(is_even)
+    def _():
         for j in range(WIDE):
             xmat[j * ROWS : (j + 1) * ROWS, :] = xak[j, :, :COLS]
             rest = xak[j, :, COLS:].astype(F32)
@@ -325,19 +342,8 @@
 
     @pl.when(is_odd)
     def _():
-        xar[w] = xr[w // 2]
-        arrived(xar.at[pl.ds(0, WIDE - 1)], x_recv.at[0], next_wide)
         for j in range(WIDE):
             xmat[j * ROWS : j * ROWS + EXL, :] = xar[j]
-
-    for s in range(MOST):
-        for offset in WIDE_OFFSETS:
-            to = wide_peer(offset)
-            remote(
-                ms.at[s, to], ma.at[s, w], own_send.at[0], own_recv.at[0], {"wide": to}
-            ).start()
-    stays = pltpu.make_async_copy(ms.at[:, w], ma.at[:, w], own_local.at[0])
-    stays.start()
 
     gram = lax.dot_general(
         xmat[...], xmat[...], (((1,), (1,)), ((), ())), preferred_element_type=F32
@@ -347,46 +353,49 @@
     gb[15] = jnp.zeros((BLK, BLK), F32)
 
     partner = {"narrow": y * 2 + 1 - c}
-    pair = remote(
-        gb.at[pl.ds((1 - c) * 8, 8)], ga, red_send.at[0], red_recv.at[0], partner
-    )
-    pair.start()
-    pair.wait_recv()
-    gh[...] = gb[pl.ds(c * 8, 8)] + ga[...]
+    red = []
+
+    def reduce_copy(src, dst, where):
+        index = len(red)
+        copy = remote(src, dst, red_send.at[index], red_recv.at[index], where)
+        copy.start()
+        red.append(copy)
+        return copy
+
+    pairs = [
+        reduce_copy(gb.at[pl.ds(i * 8 + (1 - c) * 4, 4)], ga.at[i], partner) for i in range(2)
+    ]
+    around = [((y + step) % 4, (y + 4 - step) % 4) for step in (2, 1, 3)]
     scatter = []
-    for i, step in enumerate((2, 1, 3)):
-        to = (y + step) % 4
-        copy = remote(
-            gh.at[pl.ds(to * 2, 2)],
-            gn.at[i],
-            red_send.at[1 + i],
-            red_recv.at[1 + i],
-            {"narrow": to * 2 + c},
+    for i in range(2):
+        pairs[i].wait_recv()
+        gh[i] = gb[pl.ds(i * 8 + c * 4, 4)] + ga[i]
+        scatter.append(
+            [
+                reduce_copy(gh.at[i, to], gn.at[i, step], {"narrow": to * 2 + c})
+                for step, (to, _) in enumerate(around)
+            ]
         )
-        copy.start()
-        scatter.append(copy)
-    for copy in scatter:
+    spread = []
+    for i in range(2):
+        for copy in scatter[i]:
+            copy.wait_recv()
+        mine = i * 8 + c * 4 + y
+        full[mine] = gh[i, y] + gn[i, 0] + gn[i, 1] + gn[i, 2]
+        spread.append(
+            [
+                reduce_copy(full.at[mine], full.at[mine], {"narrow": to * 2 + c})
+                for to, _ in around
+            ]
+        )
+        reduce_copy(full.at[mine], full.at[mine], partner)
+    for i in range(2):
+        for copy, (_, source) in zip(spread[i], around):
+            copy.wait_recv()
+            there = i * 8 + c * 4 + source
+            reduce_copy(full.at[there], full.at[there], partner)
+    for copy in red[11:12] + red[15:]:
         copy.wait_recv()
-    mine = pl.ds(c * 8 + y * 2, 2)
-    full[mine] = gh[pl.ds(y * 2, 2)] + gn[0] + gn[1] + gn[2]
-    gather = []
-    for i, step in enumerate((2, 1, 3)):
-        to = (y + step) % 4
-        copy = remote(
-            full.at[mine],
-            full.at[mine],
-            red_send.at[4 + i],
-            red_recv.at[4 + i],
-            {"narrow": to * 2 + c},
-        )
-        copy.start()
-        gather.append(copy)
-    for copy in gather:
-        copy.wait_recv()
-    half = pl.ds(c * 8, 8)
-    final_pair = remote(full.at[half], full.at[half], red_send.at[7], red_recv.at[7], partner)
-    final_pair.start()
-    final_pair.wait_recv()
 
     blocks = {}
     trace = jnp.zeros((1, 1), F32)
@@ -414,16 +423,17 @@
     weight = None
     for turn in range(3):
         parts = split(current)
-        cubic = split(POLY_CUBIC * current + POLY_QUINTIC * product(parts, parts))
+        square = product(parts, parts, 1 if turn == 2 else 3)
+        cubic = split(POLY_CUBIC * current + POLY_QUINTIC * square)
         if turn == 0:
             weight = jnp.where(diagonal, POLY_LINEAR, 0.0) + (
                 cubic[0].astype(F32) + cubic[1].astype(F32)
             )
         else:
-            weight = POLY_LINEAR * weight + product(cubic, split(weight))
+            weight = POLY_LINEAR * weight + product(cubic, split(weight), 2 if turn == 2 else 3)
         if turn < 2:
             half_way = POLY_LINEAR * current + product(cubic, parts)
-            current = POLY_LINEAR * half_way + product(cubic, split(half_way))
+            current = POLY_LINEAR * half_way + product(cubic, split(half_way), 3 - turn)
     wmat[...] = jnp.concatenate(split(weight * (inverse_norm * GAIN)), axis=1)
 
     layer = w // 2
@@ -500,52 +510,72 @@
     for part, source, turned in ((0, gp, tk), (1, gr, tr)):
         sent(source.at[pl.ds(0, NARROW - 1)], rot_send.at[part], next_narrow)
         sent(turned.at[pl.ds(0, NARROW - 1)], back_send.at[part], next_narrow)
-    for copy in scatter + gather + [pair, final_pair]:
+    for copy in red:
         copy.wait_send()
 
 
-def state_kernel(owner, mom, ma, out_kv, out_r, new, kv, router):
+def state_kernel(
+    owner, mom, ma_hbm, out_kv, out_r, new_hbm, kv, router, ma, new, load_sem, store_sem
+):
     w = lax.axis_index("wide")
-    s = pl.program_id(0)
-    kind = jnp.int32(0)
+    loads = [
+        pltpu.make_async_copy(ma_hbm.at[s], ma.at[s], load_sem.at[s]) for s in range(MOST)
+    ]
+    for load in loads:
+        load.start()
+    stores = [
+        pltpu.make_async_copy(new.at[s], new_hbm.at[s], store_sem.at[s]) for s in range(MOST)
+    ]
+    owners = [owner[k] for k in range(MATS)]
+    kinds = [jnp.int32(0) for _ in range(MOST)]
     for k in range(MATS):
         slot = jnp.int32(0)
         for before in range(k):
-            slot = slot + jnp.where(owner[before] == owner[k], 1, 0)
-        kind = kind + jnp.where((owner[k] == w) & (slot == s), 1 + k % 2, 0)
-
-    @pl.when(kind == 1)
-    def _():
-        for j in range(WIDE):
-            rows = slice(j * KVL, j * KVL + ROWS)
-            new[0, rows, :] = MOMENTUM_DECAY * mom[0, rows, :] + ma[0, j, :, :COLS].astype(F32)
-            rest = ma[0, j, :, COLS:].astype(F32)
-            rows = slice(j * KVL + ROWS, (j + 1) * KVL)
+            slot = slot + jnp.where(owners[before] == owners[k], 1, 0)
+        for s in range(MOST):
+            kinds[s] = kinds[s] + jnp.where((owners[k] == w) & (slot == s), 1 + k % 2, 0)
+
+    def update_state(s, kind):
+        @pl.when(kind == 1)
+        def _():
+            for j in range(WIDE):
+                rows = slice(j * KVL, j * KVL + ROWS)
+                new[s, rows, :] = MOMENTUM_DECAY * mom[s, rows, :] + ma[s, j, :, :COLS].astype(F32)
+                rest = ma[s, j, :, COLS:].astype(F32)
+                rows = slice(j * KVL + ROWS, (j + 1) * KVL)
+                for t in range(TILES):
+                    cols = slice(t * BLK, (t + 1) * BLK)
+                    new[s, rows, cols] = (
+                        MOMENTUM_DECAY * mom[s, rows, cols] + rest[t * TAIL : (t + 1) * TAIL]
+                    )
+
+        @pl.when(kind == 2)
+        def _():
+            for j in range(WIDE):
+                rows = slice(j * EXL, (j + 1) * EXL)
+                new[s, rows, :] = MOMENTUM_DECAY * mom[s, rows, :] + ma[
+                    s, j, :EXL, :COLS
+                ].astype(F32)
+            new[s, EX:, :] = jnp.zeros((KV - EX, COLS), F32)
+
+        @pl.when(kind == 0)
+        def _():
+            new[s] = jnp.zeros((KV, COLS), F32)
+
+    for s in range(MOST):
+        if s == 1:
+            router[...] = out_r[...]
             for t in range(TILES):
                 cols = slice(t * BLK, (t + 1) * BLK)
-                new[0, rows, cols] = (
-                    MOMENTUM_DECAY * mom[0, rows, cols] + rest[t * TAIL : (t + 1) * TAIL]
-                )
-
-    @pl.when(kind == 2)
-    def _():
-        for j in range(WIDE):
-            rows = slice(j * EXL, (j + 1) * EXL)
-            new[0, rows, :] = MOMENTUM_DECAY * mom[0, rows, :] + ma[0, j, :EXL, :COLS].astype(F32)
-        new[0, EX:, :] = jnp.zeros((KV - EX, COLS), F32)
-
-    @pl.when(kind == 0)
-    def _():
-        new[...] = jnp.zeros((1, KV, COLS), F32)
-
-    @pl.when(s == 0)
-    def _():
-        router[...] = out_r[...]
-        for t in range(TILES):
-            cols = slice(t * BLK, (t + 1) * BLK)
-            kv[:ROWS, :, cols] = jnp.swapaxes(out_kv[:, :, cols].astype(F32), 0, 1).astype(BF16)
-            rest = out_kv[:, :, COLS:].astype(F32)[:, t * TAIL : (t + 1) * TAIL]
-            kv[ROWS:, :, cols] = jnp.swapaxes(rest, 0, 1).astype(BF16)
+                by_row = jnp.swapaxes(out_kv[:, :, cols].astype(F32), 0, 1)
+                kv[:ROWS, :, cols] = by_row.astype(BF16)
+                rest = out_kv[:, :, COLS:].astype(F32)[:, t * TAIL : (t + 1) * TAIL]
+                kv[ROWS:, :, cols] = jnp.swapaxes(rest, 0, 1).astype(BF16)
+        loads[s].wait()
+        update_state(s, kinds[s])
+        stores[s].start()
+    for store in stores:
+        store.wait()
 
 
 def local(grad_kv, grad_router, momentum, owner):
@@ -586,9 +616,9 @@
             pltpu.VMEM((PADDED - WIDE * ROWS, COLS), F32),
             pltpu.VMEM((WIDE, ROWS, BLK), F32),
             square(16),
-            square(8),
-            square(8),
-            square(3, 2),
+            square(2, 4),
+            square(2, 4),
+            square(2, 3),
             square(16),
             pltpu.VMEM((KV, 2 * KV), BF16),
             kv_blocks(WIDE),
@@ -606,38 +636,32 @@
             dma((1,)),
             dma((1,)),
             dma((1,)),
-            dma((8,)),
-            dma((8,)),
+            dma((22,)),
+            dma((22,)),
             dma((1,)),
             dma((2,)),
         ],
         compiler_params=pltpu.CompilerParams(
-            collective_id=0, has_side_effects=True, vmem_limit_bytes=60 * 2**20
+            collective_id=0, has_side_effects=True, vmem_limit_bytes=50 * 2**20
         ),
         name="step",
     )(jnp.swapaxes(grad_kv, 0, 1), grad_router, momentum, owner)
-    whole = lambda shape: pl.BlockSpec(shape, lambda s: (0,) * len(shape))
     new_momentum, kv, router = pl.pallas_call(
         state_kernel,
-        grid=(MOST,),
         out_shape=(
             jax.ShapeDtypeStruct((MOST, KV, COLS), F32),
             jax.ShapeDtypeStruct((KVL, LAYERS, COLS), BF16),
             jax.ShapeDtypeStruct((LAYERS, EXL, COLS), BF16),
         ),
-        in_specs=[
-            smem,
-            pl.BlockSpec((1, KV, COLS), lambda s: (s, 0, 0)),
-            pl.BlockSpec((1, WIDE, ROWS, LANES), lambda s: (s, 0, 0, 0)),
-            whole((LAYERS, ROWS, LANES)),
-            whole((LAYERS, EXL, COLS)),
+        in_specs=[smem, vmem, hbm, vmem, vmem],
+        out_specs=(hbm, vmem, vmem),
+        scratch_shapes=[
+            kv_blocks(MOST, WIDE),
+            pltpu.VMEM((MOST, KV, COLS), F32),
+            dma((MOST,)),
+            dma((MOST,)),
         ],
-        out_specs=(
-            pl.BlockSpec((1, KV, COLS), lambda s: (s, 0, 0)),
-            whole((KVL, LAYERS, COLS)),
-            whole((LAYERS, EXL, COLS)),
-        ),
-        compiler_params=pltpu.CompilerParams(vmem_limit_bytes=60 * 2**20),
+        compiler_params=pltpu.CompilerParams(vmem_limit_bytes=32 * 2**20),
         name="state",
     )(owner, momentum, arrived, update_kv, update_router)
     return jnp.swapaxes(kv, 0, 1), router, new_momentum

time: 122 us -> 118 us (0.967)
  Pallas kernels: 121 us -> 112 us
  local copies, waits for them, and re-layouts: 0 us -> 4.94 us
    pallas_call x1, Pallas kernels: 113 us -> 107 us  [local(): pl.pallas_call(step_kernel, out_shape=(jax.ShapeDtypeStruct((LAYERS, ROWS...]
    unnamed x0 -> x10, local copies, waits for them, and re-layouts: none -> 4.94 us
    pallas_call x1, Pallas kernels: 8.17 us -> 4.81 us  [local(): pl.pallas_call(state_kernel, out_shape=(jax.ShapeDtypeStruct((MOST, KV, C...]
where the time goes in v3:
time: 118 us
  Pallas kernels  112 us (95%)
  local copies, waits for them, and re-layouts  4.94 us (4%)
    pallas_call x1, Pallas kernels, local(): pl.pallas_call(step_kernel, out_shape=(jax.ShapeDtypeStruct((LAYERS, ROWS...  107 us
    unnamed x10, local copies, waits for them, and re-layouts  4.94 us
    pallas_call x1, Pallas kernels, local(): pl.pallas_call(state_kernel, out_shape=(jax.ShapeDtypeStruct((MOST, KV, C...  4.81 us

profile of v3, /device:TPU:1, one launch (start us, length us, event | category | flops | bytes accessed | tf_op | source)
XLA Modules:
  0.0 118.1 jit_solution(859128298250918972)
XLA Ops:
  0.6 0.0 copy-start
  0.6 0.0 copy-start.2
  0.7 1.2 copy-done.2
  1.8 0.0 copy-start.3
  1.8 1.2 %copy-done.3 = bf16[8,24,896]{2,1,0:T(8,128)(2,1)S(1)} copy-done((bf16[8,24,896]{2,1,0:T(8,128)(2,1)S(1)}, bf16[8,24,896]{2,1,0:T(8,128)(2,1)}, u32[]{:S(2)}) %copy-start.3) | copy-done | bytes 344088
  3.1 0.0 copy-start.4
  3.1 0.7 copy-done.4
  3.7 107.5 %step.1 = (bf16[8,32,1024]{2,1,0:T(8,128)(2,1)S(1)}, bf16[8,24,896]{2,1,0:T(8,128)(2,1)S(1)}, bf16[3,16,32,1024]{3,2,1,0:T(8,128)(2,1)}) custom-call(bf16[36,8,896]{2,1,0:T(8,128)(2,1)S(1)} %bitcast.2, bf16[8,24,896]{2,1,0:T(8,128)(2,1)S(1)} %copy-done.3, f32[3,576,896]{2,1,0:T(8,128)} %mom.1, s32[16]{0:T(128)S(1)} %copy-done.4), custom_call_target="tpu_custom_call" | custom-call | tf_op jit(solution)/shard_map/step/pallas_call | solution.py:589
  111.2 0.0 copy-done
  111.2 0.0 copy-start.1
  111.2 1.9 %copy-done.1 = bf16[3,16,32,1024]{3,2,1,0:T(8,128)(2,1)S(1)} copy-done((bf16[3,16,32,1024]{3,2,1,0:T(8,128)(2,1)S(1)}, bf16[3,16,32,1024]{3,2,1,0:T(8,128)(2,1)}, u32[]{:S(2)}) %copy-start.1) | copy-done | bytes 3145752
  113.1 4.8 %state.1 = (f32[3,576,896]{2,1,0:T(8,128)}, bf16[36,8,896]{2,1,0:T(8,128)(2,1)}, bf16[8,24,896]{2,1,0:T(8,128)(2,1)}) custom-call(s32[16]{0:T(128)S(1)} %copy-done.4, f32[3,576,896]{2,1,0:T(8,128)S(1)} %copy-done, bf16[3,16,32,1024]{3,2,1,0:T(8,128)(2,1)S(1)} %copy-done.1, bf16[8,32,1024]{2,1,0:T(8,128)(2,1)S(1)} %get-tuple-element.10.out_kv, ...), custom_call_target="tpu_custom_call" | custom-call | tf_op jit(solution)/shard_map/state/pallas_call | solution.py:649
Async XLA Ops:
  0.6 110.5 %copy-start = (f32[3,576,896]{2,1,0:T(8,128)S(1)}, f32[3,576,896]{2,1,0:T(8,128)}, u32[]{:S(2)}) copy-start(f32[3,576,896]{2,1,0:T(8,128)} %mom.1) | copy-start | bytes 18579460
  0.6 1.2 %copy-start.2 = (bf16[8,36,896]{2,0,1:T(8,128)(2,1)S(1)}, bf16[8,36,896]{2,0,1:T(8,128)(2,1)}, u32[]{:S(2)}) copy-start(bf16[8,36,896]{2,0,1:T(8,128)(2,1)} %param.4) | copy-start | bytes 1548292
  1.8 1.2 %copy-start.3 = (bf16[8,24,896]{2,1,0:T(8,128)(2,1)S(1)}, bf16[8,24,896]{2,1,0:T(8,128)(2,1)}, u32[]{:S(2)}) copy-start(bf16[8,24,896]{2,1,0:T(8,128)(2,1)} %gr.1) | copy-start | bytes 1032196
  3.1 0.7 copy-start.4
  111.2 1.9 %copy-start.1 = (bf16[3,16,32,1024]{3,2,1,0:T(8,128)(2,1)S(1)}, bf16[3,16,32,1024]{3,2,1,0:T(8,128)(2,1)}, u32[]{:S(2)}) copy-start(bf16[3,16,32,1024]{3,2,1,0:T(8,128)(2,1)} %get-tuple-element.9.ma_hbm) | copy-start | bytes 9437188

commit v4 on v3

--- a/solution.py
+++ b/solution.py
@@ -46,7 +46,9 @@
     [(i, j) for i in range(4) for j in range(4) if i or j], key=lambda o: -hops(o)
 )
 NARROW_OFFSETS = [(2, 0), (2, 1), (1, 0), (3, 0), (1, 1), (3, 1), (0, 1)]
-UPPER = [(i, j) for i in range(5) for j in range(i, 5)]
+UPPER = [(i, j) for i in range(4) for j in range(i, 4)]
+HALF = BLK // 2
+PARTS = 3
 
 
 def split(value):
@@ -313,15 +315,17 @@
     @pl.when(is_even)
     def _():
         xak[w] = xk[w // 2]
-        arrived(xak.at[pl.ds(0, WIDE - 1)], x_recv.at[0], next_wide)
+        sent(xk.at[pl.ds(0, 7)], x_send.at[0], next_wide)
+        sent(xr.at[pl.ds(0, 8)], x_send.at[1], next_wide)
 
     @pl.when(is_odd)
     def _():
         xar[w] = xr[w // 2]
-        arrived(xar.at[pl.ds(0, WIDE - 1)], x_recv.at[0], next_wide)
+        sent(xk.at[pl.ds(0, 8)], x_send.at[0], next_wide)
+        sent(xr.at[pl.ds(0, 7)], x_send.at[1], next_wide)
 
     for s in range(MOST):
-        for offset in WIDE_OFFSETS:
+        for offset in WIDE_OFFSETS[::-1]:
             to = wide_peer(offset)
             remote(
                 ms.at[s, to], ma.at[s, w], own_send.at[0], own_recv.at[0], {"wide": to}
@@ -331,6 +335,7 @@
 
     @pl.when(is_even)
     def _():
+        arrived(xak.at[pl.ds(0, WIDE - 1)], x_recv.at[0], next_wide)
         for j in range(WIDE):
             xmat[j * ROWS : (j + 1) * ROWS, :] = xak[j, :, :COLS]
             rest = xak[j, :, COLS:].astype(F32)
@@ -342,6 +347,7 @@
 
     @pl.when(is_odd)
     def _():
+        arrived(xar.at[pl.ds(0, WIDE - 1)], x_recv.at[0], next_wide)
         for j in range(WIDE):
             xmat[j * ROWS : j * ROWS + EXL, :] = xar[j]
 
@@ -349,8 +355,14 @@
         xmat[...], xmat[...], (((1,), (1,)), ((), ())), preferred_element_type=F32
     )
     for b, (i, j) in enumerate(UPPER):
-        gb[b] = gram[i * BLK : (i + 1) * BLK, j * BLK : (j + 1) * BLK]
-    gb[15] = jnp.zeros((BLK, BLK), F32)
+        for side in range(2):
+            top = i * BLK + side * HALF
+            gb[2 * b + side] = gram[top : top + HALF, j * BLK : (j + 1) * BLK]
+    for j in range(4):
+        gb[20 + j] = gram[4 * BLK : 4 * BLK + HALF, j * BLK : (j + 1) * BLK]
+    corner = gram[4 * BLK : 4 * BLK + HALF, 4 * BLK :]
+    left = lax.broadcasted_iota(jnp.int32, (HALF, BLK), 1) < HALF
+    gb[1] = jnp.where(left, corner, gb[1])
 
     partner = {"narrow": y * 2 + 1 - c}
     red = []
@@ -363,11 +375,11 @@
         return copy
 
     pairs = [
-        reduce_copy(gb.at[pl.ds(i * 8 + (1 - c) * 4, 4)], ga.at[i], partner) for i in range(2)
+        reduce_copy(gb.at[pl.ds(i * 8 + (1 - c) * 4, 4)], ga.at[i], partner) for i in range(PARTS)
     ]
     around = [((y + step) % 4, (y + 4 - step) % 4) for step in (2, 1, 3)]
     scatter = []
-    for i in range(2):
+    for i in range(PARTS):
         pairs[i].wait_recv()
         gh[i] = gb[pl.ds(i * 8 + c * 4, 4)] + ga[i]
         scatter.append(
@@ -377,7 +389,8 @@
             ]
         )
     spread = []
-    for i in range(2):
+    back_to_core = []
+    for i in range(PARTS):
         for copy in scatter[i]:
             copy.wait_recv()
         mine = i * 8 + c * 4 + y
@@ -388,13 +401,13 @@
                 for to, _ in around
             ]
         )
-        reduce_copy(full.at[mine], full.at[mine], partner)
-    for i in range(2):
+        back_to_core.append(reduce_copy(full.at[mine], full.at[mine], partner))
+    for i in range(PARTS):
         for copy, (_, source) in zip(spread[i], around):
             copy.wait_recv()
             there = i * 8 + c * 4 + source
-            reduce_copy(full.at[there], full.at[there], partner)
-    for copy in red[11:12] + red[15:]:
+            back_to_core.append(reduce_copy(full.at[there], full.at[there], partner))
+    for copy in back_to_core:
         copy.wait_recv()
 
     blocks = {}
@@ -404,12 +417,23 @@
         == lax.broadcasted_iota(jnp.int32, (BLK, BLK), 1)
     )
     for b, (i, j) in enumerate(UPPER):
-        block = full[b]
+        block = jnp.concatenate([full[2 * b], full[2 * b + 1]], axis=0)
+        if b == 0:
+            lower = lax.broadcasted_iota(jnp.int32, (BLK, BLK), 0) >= HALF
+            early = lax.broadcasted_iota(jnp.int32, (BLK, BLK), 1) < HALF
+            block = jnp.where(lower & early, block.T, block)
         blocks[i, j] = block
         if i == j:
             trace = trace + jnp.sum(jnp.where(eye, block, 0.0), keepdims=True)
         else:
             blocks[j, i] = block.T
+    nothing = jnp.zeros((HALF, BLK), F32)
+    for j in range(4):
+        blocks[4, j] = jnp.concatenate([full[20 + j], nothing], axis=0)
+        blocks[j, 4] = blocks[4, j].T
+    corner = jnp.concatenate([jnp.where(left, full[1], 0.0), nothing], axis=0)
+    blocks[4, 4] = corner
+    trace = trace + jnp.sum(jnp.where(eye, corner, 0.0), keepdims=True)
     first = jnp.concatenate(
         [jnp.concatenate([blocks[i, j] for j in range(5)], axis=1) for i in range(5)], axis=0
     )[:KV, :KV]
@@ -491,8 +515,6 @@
         arrived(out_kv.at[pl.ds(0, 7)], out_recv.at[0], next_wide)
         arrived(out_r.at[pl.ds(0, 8)], out_recv.at[1], next_wide)
         sent(uk.at[pl.ds(0, 15)], out_send.at[0], next_wide)
-        sent(xk.at[pl.ds(0, 7)], x_send.at[0], next_wide)
-        sent(xr.at[pl.ds(0, 8)], x_send.at[1], next_wide)
 
     @pl.when(is_odd)
     def _():
@@ -500,8 +522,6 @@
         arrived(out_kv.at[pl.ds(0, 8)], out_recv.at[0], next_wide)
         arrived(out_r.at[pl.ds(0, 7)], out_recv.at[1], next_wide)
         sent(ur.at[pl.ds(0, 15)], out_send.at[0], next_wide)
-        sent(xk.at[pl.ds(0, 8)], x_send.at[0], next_wide)
-        sent(xr.at[pl.ds(0, 7)], x_send.at[1], next_wide)
 
     arrived(ma.at[:, pl.ds(0, WIDE - 1)], own_recv.at[0], next_wide)
     stays.wait()
@@ -585,7 +605,7 @@
     dma = pltpu.SemaphoreType.DMA
     kv_blocks = lambda *count: pltpu.VMEM(count + (ROWS, LANES), BF16)
     r_blocks = lambda count: pltpu.VMEM((count, EXL, COLS), BF16)
-    square = lambda *count: pltpu.VMEM(count + (BLK, BLK), F32)
+    pieces = lambda *count: pltpu.VMEM(count + (HALF, BLK), F32)
     update_kv, update_router, arrived = pl.pallas_call(
         step_kernel,
         out_shape=(
@@ -615,11 +635,11 @@
             pltpu.VMEM((PADDED, COLS), BF16),
             pltpu.VMEM((PADDED - WIDE * ROWS, COLS), F32),
             pltpu.VMEM((WIDE, ROWS, BLK), F32),
-            square(16),
-            square(2, 4),
-            square(2, 4),
-            square(2, 3),
-            square(16),
+            pieces(24),
+            pieces(PARTS, 4),
+            pieces(PARTS, 4),
+            pieces(PARTS, 3),
+            pieces(24),
             pltpu.VMEM((KV, 2 * KV), BF16),
             kv_blocks(WIDE),
             r_blocks(WIDE),
@@ -636,8 +656,8 @@
             dma((1,)),
             dma((1,)),
             dma((1,)),
-            dma((22,)),
-            dma((22,)),
+            dma((11 * PARTS,)),
+            dma((11 * PARTS,)),
             dma((1,)),
             dma((2,)),
         ],

time: 118 us -> 116 us (0.983)
  Pallas kernels: 112 us -> 110 us
    pallas_call x1, Pallas kernels: 107 us -> 105 us  [local(): pl.pallas_call(step_kernel, out_shape=(jax.ShapeDtypeStruct((LAYERS, ROWS...]
where the time goes in v4:
time: 116 us
  Pallas kernels  110 us (95%)
  local copies, waits for them, and re-layouts  4.94 us (4%)
    pallas_call x1, Pallas kernels, local(): pl.pallas_call(step_kernel, out_shape=(jax.ShapeDtypeStruct((LAYERS, ROWS...  105 us
    unnamed x10, local copies, waits for them, and re-layouts  4.94 us
    pallas_call x1, Pallas kernels, local(): pl.pallas_call(state_kernel, out_shape=(jax.ShapeDtypeStruct((MOST, KV, C...  4.73 us

profile of v4, /device:TPU:1, one launch (start us, length us, event | category | flops | bytes accessed | tf_op | source)
XLA Modules:
  0.0 115.8 jit_solution(697742844035822765)
XLA Ops:
  0.6 0.0 copy-start
  0.6 0.0 copy-start.2
  0.7 1.2 %copy-done.2 = bf16[8,36,896]{2,0,1:T(8,128)(2,1)S(1)} copy-done((bf16[8,36,896]{2,0,1:T(8,128)(2,1)S(1)}, bf16[8,36,896]{2,0,1:T(8,128)(2,1)}, u32[]{:S(2)}) %copy-start.2) | copy-done | bytes 516120
  1.8 0.0 copy-start.3
  1.8 1.2 %copy-done.3 = bf16[8,24,896]{2,1,0:T(8,128)(2,1)S(1)} copy-done((bf16[8,24,896]{2,1,0:T(8,128)(2,1)S(1)}, bf16[8,24,896]{2,1,0:T(8,128)(2,1)}, u32[]{:S(2)}) %copy-start.3) | copy-done | bytes 344088
  3.1 0.0 copy-start.4
  3.1 0.7 copy-done.4
  3.7 105.2 %step.1 = (bf16[8,32,1024]{2,1,0:T(8,128)(2,1)S(1)}, bf16[8,24,896]{2,1,0:T(8,128)(2,1)S(1)}, bf16[3,16,32,1024]{3,2,1,0:T(8,128)(2,1)}) custom-call(bf16[36,8,896]{2,1,0:T(8,128)(2,1)S(1)} %bitcast.2, bf16[8,24,896]{2,1,0:T(8,128)(2,1)S(1)} %copy-done.3, f32[3,576,896]{2,1,0:T(8,128)} %mom.1, s32[16]{0:T(128)S(1)} %copy-done.4), custom_call_target="tpu_custom_call" | custom-call | tf_op jit(solution)/shard_map/step/pallas_call | solution.py:609
  108.9 0.0 copy-done
  109.0 0.0 copy-start.1
  109.0 1.9 %copy-done.1 = bf16[3,16,32,1024]{3,2,1,0:T(8,128)(2,1)S(1)} copy-done((bf16[3,16,32,1024]{3,2,1,0:T(8,128)(2,1)S(1)}, bf16[3,16,32,1024]{3,2,1,0:T(8,128)(2,1)}, u32[]{:S(2)}) %copy-start.1) | copy-done | bytes 3145752
  110.8 4.7 %state.1 = (f32[3,576,896]{2,1,0:T(8,128)}, bf16[36,8,896]{2,1,0:T(8,128)(2,1)}, bf16[8,24,896]{2,1,0:T(8,128)(2,1)}) custom-call(s32[16]{0:T(128)S(1)} %copy-done.4, f32[3,576,896]{2,1,0:T(8,128)S(1)} %copy-done, bf16[3,16,32,1024]{3,2,1,0:T(8,128)(2,1)S(1)} %copy-done.1, bf16[8,32,1024]{2,1,0:T(8,128)(2,1)S(1)} %get-tuple-element.10.out_kv, ...), custom_call_target="tpu_custom_call" | custom-call | tf_op jit(solution)/shard_map/state/pallas_call | solution.py:669
Async XLA Ops:
  0.6 108.3 %copy-start = (f32[3,576,896]{2,1,0:T(8,128)S(1)}, f32[3,576,896]{2,1,0:T(8,128)}, u32[]{:S(2)}) copy-start(f32[3,576,896]{2,1,0:T(8,128)} %mom.1) | copy-start | bytes 18579460
  0.6 1.2 %copy-start.2 = (bf16[8,36,896]{2,0,1:T(8,128)(2,1)S(1)}, bf16[8,36,896]{2,0,1:T(8,128)(2,1)}, u32[]{:S(2)}) copy-start(bf16[8,36,896]{2,0,1:T(8,128)(2,1)} %param.4) | copy-start | bytes 1548292
  1.8 1.2 %copy-start.3 = (bf16[8,24,896]{2,1,0:T(8,128)(2,1)S(1)}, bf16[8,24,896]{2,1,0:T(8,128)(2,1)}, u32[]{:S(2)}) copy-start(bf16[8,24,896]{2,1,0:T(8,128)(2,1)} %gr.1) | copy-start | bytes 1032196
  3.1 0.7 copy-start.4
  109.0 1.9 %copy-start.1 = (bf16[3,16,32,1024]{3,2,1,0:T(8,128)(2,1)S(1)}, bf16[3,16,32,1024]{3,2,1,0:T(8,128)(2,1)}, u32[]{:S(2)}) copy-start(bf16[3,16,32,1024]{3,2,1,0:T(8,128)(2,1)} %get-tuple-element.9.ma_hbm) | copy-start | bytes 9437188

commit v5 on v4

--- a/solution.py
+++ b/solution.py
@@ -195,7 +195,7 @@
         msend[s, :, :, COLS:] = tails[...].astype(BF16)
 
     def send_momentum(s):
-        for offset in WIDE_OFFSETS:
+        for offset in WIDE_OFFSETS[::-1]:
             to = wide_peer(offset)
             remote(
                 msend.at[s, to], marr.at[w, s], mom_send.at[0], mom_recv.at[0], {"wide": to}
@@ -281,8 +281,9 @@
     lax.fori_loop(0, WIDE, stage, 0)
     arrived(marr.at[pl.ds(0, WIDE - 1)], mom_recv.at[0], next_wide)
 
-    def push(layer, carry):
-        for part, (source, target) in enumerate(((mk, xk), (mr, xr))):
+    def push(step, carry):
+        layer = (w // 2 + 1 + step) % LAYERS
+        for part, (source, target, landing) in enumerate(((mk, xk, xak), (mr, xr, xar))):
             k = 2 * layer + part
             held = marr[owner[k], jnp.minimum(slot_ref[k], MOST - 1)]
             if part:
@@ -290,24 +291,16 @@
             fresh = source[layer].astype(F32)
             state = MOMENTUM_DECAY * held.astype(F32) + fresh
             target[layer] = (fresh + MOMENTUM_DECAY * state).astype(BF16)
+
+            @pl.when(k != w)
+            def _():
+                remote(
+                    target.at[layer], landing.at[w], x_send.at[part], x_recv.at[0], {"wide": k}
+                ).start()
+
         return carry
 
     lax.fori_loop(0, LAYERS, push, 0)
-
-    for offset in WIDE_OFFSETS:
-        to = wide_peer(offset)
-
-        @pl.when(to % 2 == 0)
-        def _():
-            remote(
-                xk.at[to // 2], xak.at[w], x_send.at[0], x_recv.at[0], {"wide": to}
-            ).start()
-
-        @pl.when(to % 2 == 1)
-        def _():
-            remote(
-                xr.at[to // 2], xar.at[w], x_send.at[1], x_recv.at[0], {"wide": to}
-            ).start()
 
     xmat[...] = jnp.zeros(xmat.shape, BF16)
     xtail[...] = jnp.zeros(xtail.shape, F32)

time: 116 us -> 115 us (level)
  Pallas kernels: 110 us -> 108 us
    pallas_call x1, Pallas kernels: 105 us -> 104 us  [local(): pl.pallas_call(step_kernel, out_shape=(jax.ShapeDtypeStruct((LAYERS, ROWS...]
where the time goes in v5:
time: 115 us; the launch traced here: 114 us
  Pallas kernels  108 us (94%)
  local copies, waits for them, and re-layouts  4.94 us (4%)
    pallas_call x1, Pallas kernels, local(): pl.pallas_call(step_kernel, out_shape=(jax.ShapeDtypeStruct((LAYERS, ROWS...  104 us
    unnamed x10, local copies, waits for them, and re-layouts  4.94 us
    pallas_call x1, Pallas kernels, local(): pl.pallas_call(state_kernel, out_shape=(jax.ShapeDtypeStruct((MOST, KV, C...  4.81 us

profile of v5, /device:TPU:1, one launch (start us, length us, event | category | flops | bytes accessed | tf_op | source)
XLA Modules:
  0.0 114.2 jit_solution(12442904765879742612)
XLA Ops:
  0.6 0.0 copy-start
  0.6 0.0 copy-start.2
  0.7 1.2 %copy-done.2 = bf16[8,36,896]{2,0,1:T(8,128)(2,1)S(1)} copy-done((bf16[8,36,896]{2,0,1:T(8,128)(2,1)S(1)}, bf16[8,36,896]{2,0,1:T(8,128)(2,1)}, u32[]{:S(2)}) %copy-start.2) | copy-done | bytes 516120
  1.8 0.0 copy-start.3
  1.8 1.2 %copy-done.3 = bf16[8,24,896]{2,1,0:T(8,128)(2,1)S(1)} copy-done((bf16[8,24,896]{2,1,0:T(8,128)(2,1)S(1)}, bf16[8,24,896]{2,1,0:T(8,128)(2,1)}, u32[]{:S(2)}) %copy-start.3) | copy-done | bytes 344088
  3.1 0.0 copy-start.4
  3.1 0.7 copy-done.4
  3.7 103.6 %step.1 = (bf16[8,32,1024]{2,1,0:T(8,128)(2,1)S(1)}, bf16[8,24,896]{2,1,0:T(8,128)(2,1)S(1)}, bf16[3,16,32,1024]{3,2,1,0:T(8,128)(2,1)}) custom-call(bf16[36,8,896]{2,1,0:T(8,128)(2,1)S(1)} %bitcast.2, bf16[8,24,896]{2,1,0:T(8,128)(2,1)S(1)} %copy-done.3, f32[3,576,896]{2,1,0:T(8,128)} %mom.1, s32[16]{0:T(128)S(1)} %copy-done.4), custom_call_target="tpu_custom_call" | custom-call | tf_op jit(solution)/shard_map/step/pallas_call | solution.py:602
  107.3 0.0 copy-done
  107.3 0.0 copy-start.1
  107.4 1.9 %copy-done.1 = bf16[3,16,32,1024]{3,2,1,0:T(8,128)(2,1)S(1)} copy-done((bf16[3,16,32,1024]{3,2,1,0:T(8,128)(2,1)S(1)}, bf16[3,16,32,1024]{3,2,1,0:T(8,128)(2,1)}, u32[]{:S(2)}) %copy-start.1) | copy-done | bytes 3145752
  109.2 4.8 %state.1 = (f32[3,576,896]{2,1,0:T(8,128)}, bf16[36,8,896]{2,1,0:T(8,128)(2,1)}, bf16[8,24,896]{2,1,0:T(8,128)(2,1)}) custom-call(s32[16]{0:T(128)S(1)} %copy-done.4, f32[3,576,896]{2,1,0:T(8,128)S(1)} %copy-done, bf16[3,16,32,1024]{3,2,1,0:T(8,128)(2,1)S(1)} %copy-done.1, bf16[8,32,1024]{2,1,0:T(8,128)(2,1)S(1)} %get-tuple-element.10.out_kv, ...), custom_call_target="tpu_custom_call" | custom-call | tf_op jit(solution)/shard_map/state/pallas_call | solution.py:662
Async XLA Ops:
  0.6 106.7 %copy-start = (f32[3,576,896]{2,1,0:T(8,128)S(1)}, f32[3,576,896]{2,1,0:T(8,128)}, u32[]{:S(2)}) copy-start(f32[3,576,896]{2,1,0:T(8,128)} %mom.1) | copy-start | bytes 18579460
  0.6 1.2 %copy-start.2 = (bf16[8,36,896]{2,0,1:T(8,128)(2,1)S(1)}, bf16[8,36,896]{2,0,1:T(8,128)(2,1)}, u32[]{:S(2)}) copy-start(bf16[8,36,896]{2,0,1:T(8,128)(2,1)} %param.4) | copy-start | bytes 1548292
  1.8 1.2 %copy-start.3 = (bf16[8,24,896]{2,1,0:T(8,128)(2,1)S(1)}, bf16[8,24,896]{2,1,0:T(8,128)(2,1)}, u32[]{:S(2)}) copy-start(bf16[8,24,896]{2,1,0:T(8,128)(2,1)} %gr.1) | copy-start | bytes 1032196
  3.1 0.7 copy-start.4
  107.3 1.9 %copy-start.1 = (bf16[3,16,32,1024]{3,2,1,0:T(8,128)(2,1)S(1)}, bf16[3,16,32,1024]{3,2,1,0:T(8,128)(2,1)}, u32[]{:S(2)}) copy-start(bf16[3,16,32,1024]{3,2,1,0:T(8,128)(2,1)} %get-tuple-element.9.ma_hbm) | copy-start | bytes 9437188
